TPU v7x, 256 devices: a whole 4x4x8 slice. The times are simulated.
256 devices in a mesh: row: 8 (over y_lo, x), col: 32 (over z, y_hi, core).
Axes of the slice: x: 4, y: 4 (y_hi: 2, y_lo: 2; y = y_hi * 2 + y_lo), z: 8, core: 2. Of those that a mesh axis runs over, the one named last changes fastest.
Arguments:
- counts: int32 [2, 16384, 16384], P(None, 'row', 'col'), may hold values from 0 to 199, as said below
- row_embed: float32 [2, 16384, 256], P(None, ('row', 'col')), may hold values from -1.5 to 1.5
- col_embed: float32 [2, 16384, 256], P(None, ('col', 'row')), may hold values from -1.5 to 1.5
- row_marg: int32 [2, 16384], P(None, ('row', 'col')), may hold values from 2000 to 59999
- col_marg: int32 [2, 16384], P(None, ('col', 'row')), may hold values from 2000 to 59999
- row_accum: float32 [2, 16384, 256], P(None, ('row', 'col')), may hold values from 1000 to 100000
- col_accum: float32 [2, 16384, 256], P(None, ('col', 'row')), may hold values from 1000 to 100000
Outputs:
- new_rows: float32 [2, 16384, 256], P(None, ('row', 'col'))
- new_cols: float32 [2, 16384, 256], P(None, ('col', 'row'))
Inputs may be any that keep to these rules, and one draw needn't show every extreme that they name: `counts`: about half of the cells are zero.
All inputs are finite; a program needn't handle non-finite values.
Results may differ from a plain program's by a relative error of at most 0.0075.
Values may be sent and summed in bfloat16 or wider, within the bound.
A program may use at most 64 MiB of HBM per device.

v0:
```python
import jax
import jax.numpy as jnp
from jax import lax
from jax.sharding import PartitionSpec as P

LOG_TOTAL = 20.0
LEARN_RATE = 1.0


def cell_grads(counts, rows_half, cols_half, row_counts, col_counts):
    scores = jnp.einsum("srd,scd->src", rows_half, cols_half, preferred_element_type=jnp.float32)
    pmi_zero = (
        LOG_TOTAL
        - jnp.log(row_counts.astype(jnp.float32))[:, :, None]
        - jnp.log(col_counts.astype(jnp.float32))[:, None, :]
    )
    counts_real = counts.astype(jnp.float32)
    pmi_full = jnp.log(jnp.maximum(counts_real, 1.0)) + pmi_zero
    confidence = 0.1 + 0.25 * jnp.sqrt(counts_real)
    return jnp.where(
        counts > 0, confidence * (scores - pmi_full), jax.nn.sigmoid(scores - pmi_zero)
    ).astype(jnp.bfloat16)


def adagrad(weights, accum, gradient):
    return weights - LEARN_RATE * gradient / jnp.sqrt(accum + gradient * gradient)


def process(counts, row_embed, col_embed, row_marg, col_marg, row_accum, col_accum):
    rows_half, row_counts = (
        lax.all_gather(row_embed.astype(jnp.bfloat16), "col", axis=1, tiled=True),
        lax.all_gather(row_marg, "col", axis=1, tiled=True),
    )
    cols_half, col_counts = (
        lax.all_gather(col_embed.astype(jnp.bfloat16), "row", axis=1, tiled=True),
        lax.all_gather(col_marg, "row", axis=1, tiled=True),
    )
    grads = cell_grads(counts, rows_half, cols_half, row_counts, col_counts)
    row_terms = jnp.einsum("src,scd->srd", grads, cols_half, preferred_element_type=jnp.float32)
    col_terms = jnp.einsum("src,srd->scd", grads, rows_half, preferred_element_type=jnp.float32)
    col_owned = lax.psum_scatter(col_terms, "row", scatter_dimension=1, tiled=True)
    row_owned = lax.psum_scatter(row_terms, "col", scatter_dimension=1, tiled=True)
    return (adagrad(row_embed, row_accum, row_owned), adagrad(col_embed, col_accum, col_owned))


def local(counts, row_embed, col_embed, row_marg, col_marg, row_accum, col_accum):
    row_results = []
    col_results = []
    for which_shard in range(counts.shape[0]):
        upper = which_shard + 1
        new_row, new_col = process(
            counts[which_shard:upper],
            row_embed[which_shard:upper],
            col_embed[which_shard:upper],
            row_marg[which_shard:upper],
            col_marg[which_shard:upper],
            row_accum[which_shard:upper],
            col_accum[which_shard:upper],
        )
        row_results.append(new_row)
        col_results.append(new_col)
    return (jnp.concatenate(row_results, 0), jnp.concatenate(col_results, 0))


def solution(mesh):
    return jax.shard_map(
        local,
        mesh=mesh,
        in_specs=(
            P(None, "row", "col"),
            P(None, ("row", "col"), None),
            P(None, ("col", "row"), None),
            P(None, ("row", "col")),
            P(None, ("col", "row")),
            P(None, ("row", "col"), None),
            P(None, ("col", "row"), None),
        ),
        out_specs=(P(None, ("row", "col"), None), P(None, ("col", "row"), None)),
        check_vma=False,
    )
```

profile of v0, /device:TPU:8, one launch (start us, length us, event | category | flops | bytes accessed | tf_op | source)
XLA Modules:
  0.0 554.7 jit_solution(695792761460576588)
XLA Ops:
  7.2 1.5 fusion.25
  9.5 1.3 dynamic-slice.1
  10.8 1.3 dynamic-slice
  13.4 0.8 bitcast_dynamic-update-slice_fusion
  14.9 10.9 %all-reduce.5 = (s32[512]{0:T(512)S(1)}, s32[512]{0:T(512)S(1)}) all-reduce(s32[512]{0:T(512)S(1)} %bitcast_dynamic-update-slice_fusion, s32[512]{0:T(512)S(1)} %bitcast_dynamic-update-slice_fusion.2), channel_id=1, replica_groups=mesh['row'=8,'col'=32] {'row'}, use_global_device_ids=true, to_apply=%add.3 | all-reduce | flops 1024 | bytes 8192
  25.9 0.8 bitcast_dynamic-update-slice_fusion.1
  26.7 0.8 bitcast_dynamic-update-slice_fusion.3
  27.4 0.9 fusion.24
  28.3 28.5 %all_gather.25 = bf16[1,512,256]{2,1,0:T(8,128)(2,1)S(1)} all-gather(bf16[1,64,256]{2,1,0:T(8,128)(2,1)S(1)} %get-tuple-element.10), channel_id=1, replica_groups=mesh['row'=8,'col'=32] {'row'}, dimensions={1}, use_global_device_ids=true | all-gather | bytes 294912 | tf_op jit(solution)/shard_map/all_gather | solution.py:35
  56.8 131.3 %all-reduce.4 = (s32[2048]{0:T(1024)S(1)}, s32[2048]{0:T(1024)S(1)}) all-reduce(s32[2048]{0:T(1024)S(1)} %bitcast_dynamic-update-slice_fusion.1, s32[2048]{0:T(1024)S(1)} %bitcast_dynamic-update-slice_fusion.3), channel_id=1, replica_groups=mesh['row'=8,'col'=32] {'col'}, use_global_device_ids=true, to_apply=%add.2 | all-reduce | flops 4096 | bytes 32768
  188.1 28.5 %all_gather.29 = bf16[1,512,256]{2,1,0:T(8,128)(2,1)S(1)} all-gather(bf16[1,64,256]{2,1,0:T(8,128)(2,1)S(1)} %get-tuple-element.11), channel_id=1, replica_groups=mesh['row'=8,'col'=32] {'row'}, dimensions={1}, use_global_device_ids=true | all-gather | bytes 294912 | tf_op jit(solution)/shard_map/all_gather | solution.py:35
  216.7 5.6 %fusion = bf16[1,2048,512]{2,1,0:T(8,128)(2,1)S(1)} fusion(s32[2,2048,512]{2,1,0:T(8,128)} %param.7, f32[2048]{0:T(1024)S(1)} %log_subtract_fusion, f32[512]{0:T(512)S(1)} %convert_log_fusion, bf16[1,2048,256]{2,1,0:T(8,128)(2,1)} %all-gather.5.cloned.1.call-done, bf16[1,512,256]{2,1,0:T(8,128)(2,1)S(1)} %all_gather.29), kind=kOutput, calls=%fused_computation.1 | convolution fusion | flops 553648128 | bytes 7622656 | tf_op jit(solution)/shard_map/srd,scd->src/dot_general | solution.py:11
  222.3 1.5 fusion.13
  224.0 5.6 %fusion.2 = bf16[1,2048,512]{2,1,0:T(8,128)(2,1)S(1)} fusion(s32[2,2048,512]{2,1,0:T(8,128)} %param.7, f32[2048]{0:T(1024)S(1)} %log_subtract_fusion.1, f32[512]{0:T(512)S(1)} %convert_log_fusion.1, bf16[1,2048,256]{2,1,0:T(8,128)(2,1)} %all-gather.3.cloned.1.call-done, bf16[1,512,256]{2,1,0:T(8,128)(2,1)S(1)} %all_gather.25), kind=kOutput, calls=%fused_computation.5 | convolution fusion | flops 553648128 | bytes 7622656 | tf_op jit(solution)/shard_map/srd,scd->src/dot_general | solution.py:11
  229.6 1.3 copy-done
  230.9 1.5 fusion.10
  232.5 2.0 convolution_bitcast_fusion
  234.7 3.7 convolution_bitcast_fusion.1
  238.5 22.0 %reduce-scatter.11.cloned.1.call-done = f32[1,64,256]{2,1,0:T(8,128)} async-done(((f32[1,512,256]{2,1,0:T(8,128)}), f32[1,64,256]{2,1,0:T(8,128)}) %reduce-scatter.11.cloned.1.call-update) | async-done | bytes 65552 | tf_op jit(solution)/shard_map/reduce_scatter | solution.py:41
  260.4 41.7 %reduce-scatter.9.cloned.1.call-done = f32[1,64,256]{2,1,0:T(8,128)} async-done(((f32[1,512,256]{2,1,0:T(8,128)}), f32[1,64,256]{2,1,0:T(8,128)}) %reduce-scatter.9.cloned.1.call-update) | async-done | bytes 65552 | tf_op jit(solution)/shard_map/reduce_scatter | solution.py:41
  302.1 0.9 multiply_subtract_fusion.1
  303.7 120.7 %reduce-scatter.7.cloned.1.call-done = f32[1,64,256]{2,1,0:T(8,128)} async-done(((f32[1,2048,256]{2,1,0:T(8,128)}), f32[1,64,256]{2,1,0:T(8,128)}) %reduce-scatter.7.cloned.1.call-update) | async-done | bytes 65552 | tf_op jit(solution)/shard_map/reduce_scatter | solution.py:42
  424.4 121.9 %reduce-scatter.5.cloned.1.call-done = f32[1,64,256]{2,1,0:T(8,128)} async-done(((f32[1,2048,256]{2,1,0:T(8,128)}), f32[1,64,256]{2,1,0:T(8,128)}) %reduce-scatter.5.cloned.1.call-update) | async-done | bytes 65552 | tf_op jit(solution)/shard_map/reduce_scatter | solution.py:42
  546.3 0.9 multiply_subtract_fusion.3
  (38 shorter events, 3.2 us)
Async XLA Ops:
  7.2 209.5 %all-gather.5.cloned.1.call-start = ((), (), s32[]{:S(2)}) async-start(), calls=%async_computation.6 | async-start | bytes 1081344 | tf_op jit(solution)/shard_map/all_gather | solution.py:31
  8.7 215.2 %all-gather.3.cloned.1.call-start = ((), (), s32[]{:S(2)}) async-start(), calls=%async_computation.4 | async-start | bytes 1081344 | tf_op jit(solution)/shard_map/all_gather | solution.py:31
  9.5 251.0 %reduce-scatter.11.cloned.1.call-start = ((), (), s32[]{:S(2)}) async-start(), calls=%async_computation.9 | async-start | bytes 589824 | tf_op jit(solution)/shard_map/reduce_scatter | solution.py:41
  216.7 5.6 %copy-start.2 = (bf16[1,2048,256]{2,1,0:T(8,128)(2,1)S(1)}, bf16[1,2048,256]{2,1,0:T(8,128)(2,1)}, u32[]{:S(2)}) copy-start(bf16[1,2048,256]{2,1,0:T(8,128)(2,1)} %all-gather.5.cloned.1.call-done) | copy-start | bytes 3145732
  223.9 78.2 %reduce-scatter.9.cloned.1.call-start = ((), (), s32[]{:S(2)}) async-start(), calls=%async_computation.8 | async-start | bytes 589824 | tf_op jit(solution)/shard_map/reduce_scatter | solution.py:41
  224.0 7.0 %copy-start.1 = (bf16[1,2048,256]{2,1,0:T(8,128)(2,1)S(1)}, bf16[1,2048,256]{2,1,0:T(8,128)(2,1)}, u32[]{:S(2)}) copy-start(bf16[1,2048,256]{2,1,0:T(8,128)(2,1)} %all-gather.3.cloned.1.call-done) | copy-start | bytes 3145732
  229.6 1.3 copy-start
  232.5 191.9 %reduce-scatter.7.cloned.1.call-start = ((), (), s32[]{:S(2)}) async-start(), calls=%async_computation.7 | async-start | bytes 2162688 | tf_op jit(solution)/shard_map/reduce_scatter | solution.py:42
  234.6 67.5 %copy-start.3 = (f32[2,64,256]{2,1,0:T(8,128)S(1)}, f32[2,64,256]{2,1,0:T(8,128)}, u32[]{:S(2)}) copy-start(f32[2,64,256]{2,1,0:T(8,128)} %param.9) | copy-start | bytes 393220
  234.6 67.5 %copy-start.5 = (f32[2,64,256]{2,1,0:T(8,128)S(1)}, f32[2,64,256]{2,1,0:T(8,128)}, u32[]{:S(2)}) copy-start(f32[2,64,256]{2,1,0:T(8,128)} %param.13) | copy-start | bytes 393220
  234.6 311.7 %copy-start.4 = (f32[2,64,256]{2,1,0:T(8,128)S(1)}, f32[2,64,256]{2,1,0:T(8,128)}, u32[]{:S(2)}) copy-start(f32[2,64,256]{2,1,0:T(8,128)} %param.8) | copy-start | bytes 393220
  234.6 311.7 %copy-start.6 = (f32[2,64,256]{2,1,0:T(8,128)S(1)}, f32[2,64,256]{2,1,0:T(8,128)}, u32[]{:S(2)}) copy-start(f32[2,64,256]{2,1,0:T(8,128)} %param.12) | copy-start | bytes 393220
  234.6 311.6 %reduce-scatter.5.cloned.1.call-start = ((), (), s32[]{:S(2)}) async-start(), calls=%async_computation.5 | async-start | bytes 2162688 | tf_op jit(solution)/shard_map/reduce_scatter | solution.py:42
Sparse Core Ops, SparseCore 0:
  11.4 79.5 all-gather.4
  94.3 74.3 all-gather.2
  224.0 36.3 reduce-scatter.10
  263.0 39.1 reduce-scatter.8
  306.1 118.2 reduce-scatter.6
  429.0 117.2 reduce-scatter.4
where the time goes:
time: 556 us; the launch traced here: 555 us
  waiting for transfers between devices  307 us (55%)
  blocking collectives  199 us (36%)
  matrix products  20.1 us (4%)
  between operations  15.5 us (3%)
  local copies, waits for them, and re-layouts  9.44 us (2%)
    reduce_scatter x2, waiting for transfers between devices, process(): lax.psum_scatter(row_terms, 'col', scatter_dimension=1, tiled=True)  243 us
    unnamed x2, blocking collectives  142 us
    reduce_scatter x2, waiting for transfers between devices, process(): lax.psum_scatter(col_terms, 'row', scatter_dimension=1, tiled=True)  63.7 us
    all_gather x2, blocking collectives, process(): lax.all_gather(col_embed.astype(jnp.bfloat16), 'row', axis=1, tiled=True)  57 us
    dot_general x2, matrix products, cell_grads(): jnp.einsum('srd,scd->src', rows_half, cols_half, preferred_element_type=j...  11.2 us
  transfers between devices with their start and end apart: 6, of which 4 were waited for; matrix products, arithmetic and copies ran while one was open for 5% of the time, Pallas kernels for 0%

commit v1 on v0

v1 whole, which is shorter than its diff:
```python
import functools

import jax
import jax.numpy as jnp
from jax import lax
from jax.experimental import pallas as pl
from jax.experimental.pallas import tpu as pltpu
from jax.sharding import PartitionSpec as P

MESH = pl.DeviceIdType.MESH
F32 = jnp.float32
BF16 = jnp.bfloat16
NT = (((1,), (1,)), ((), ()))
NN = (((1,), (0,)), ((), ()))
TN = (((0,), (0,)), ((), ()))


def dot(a, b, dims):
    return lax.dot_general(a, b, dims, preferred_element_type=F32)


def adagrad(w, a, g):
    return w - g / jnp.sqrt(a + g * g)


def kernel(
    NZ, XN, B, D, CN,
    counts, re_h, ce_h, rm_h, cm_h, nr, nc,
    re, ce, rm, cm,
    cnt, rows, cols, colsT, RM, CM, LRB, LC, PA, PB, RP, OWN, CPT, CP,
    CS, CR, RSp, RSm, RRp, RRm, YS, YR, VR, Q1s, Q1r, Q2s, Q2r, Q3s, Q3r, VC,
    s_in, s_cnt, s_all, r_a, r_b, r_far, r_core, r_col, r_mz, s_mz, r_mo, s_mo, r_nx, s_nx, r_cr, r_rp, r_rm, r_y, r_q,
):
    H = NZ // 2
    NS = 2
    row = lax.axis_index("row")
    col = lax.axis_index("col")
    x = lax.rem(row, XN)
    yl = row // XN
    z = col // 4
    yh = lax.rem(col // 2, 2)
    c = lax.rem(col, 2)
    oc = 1 - c
    xp = lax.rem(x + 1, XN)
    xm = lax.rem(x + XN - 1, XN)
    x2 = lax.rem(x + 2, XN)
    zp = lax.rem(z + 1, NZ)
    zm = lax.rem(z + NZ - 1, NZ)
    to_core = (row, col + 1 - 2 * c)
    to_yh = (row, col + 2 - 4 * yh)
    to_zp = (row, zp * 4 + yh * 2 + c)
    to_zm = (row, zm * 4 + yh * 2 + c)
    to_yl = ((1 - yl) * XN + x, col)
    to_xp = (yl * XN + xp, col)
    to_xm = (yl * XN + xm, col)
    to_diag = (row, col + 1 - 2 * c + 2 - 4 * yh)
    to_x2 = (yl * XN + x2, col)
    r_own = yl * XN + x
    r_oth = (1 - yl) * XN + x

    def place(r):
        return 0 if r == 0 else 2 * r - 1 if r > 0 or r == -H else -2 * r

    def place_of(r):
        return place(H) if r == -H else place(r)

    def span(d):
        return (2 * d - 1, 2) if 0 < d < H else (place_of(d), 1)

    rel = [0]
    for d in range(1, H):
        rel += [d, -d]
    rel += [H]

    def to_z(r):
        return (row, lax.rem(z + r + NZ, NZ) * 4 + yh * 2 + c)

    small = []
    total = [0]

    def send(src, dst, rsem, dev, blocks):
        pltpu.make_async_remote_copy(
            src_ref=src, dst_ref=dst, send_sem=s_all, recv_sem=rsem, device_id=dev, device_id_type=MESH
        ).start()
        total[0] += blocks

    def send_small(src, dst, ssem, rsem, dev):
        copy = pltpu.make_async_remote_copy(
            src_ref=src, dst_ref=dst, send_sem=ssem, recv_sem=rsem, device_id=dev, device_id_type=MESH
        )
        copy.start()
        small.append(copy)

    def arrive(dst, rsem):
        pltpu.make_async_copy(dst, dst, rsem).wait()

    own_in = [
        pltpu.make_async_copy(src, dst, s_in.at[i])
        for i, (src, dst) in enumerate(((rm_h, rm), (cm_h, cm), (re_h, re), (ce_h, ce)))
    ]
    for copy in own_in:
        copy.start()

    def count_copy(q, r=0):
        zc = lax.rem(z + r + NZ, NZ)
        at = pl.ds(q * 4 * B, 4 * B)
        return pltpu.make_async_copy(counts.at[q // NZ, zc], cnt.at[at], s_cnt.at[q])

    for s in range(NS):
        for p in range(NZ):
            count_copy(s * NZ + p, rel[p]).start()

    for copy in own_in:
        copy.wait()
    for s in range(NS):
        rows[s, 0, yh, c] = re[s].astype(BF16)
        cols[s, r_own] = ce[s].astype(BF16)
    mine_r = jnp.concatenate([rm[0:1, :], rm[1:2, :]], axis=1).astype(F32)
    mine_c = jnp.concatenate([cm[0:1, :], cm[1:2, :]], axis=1).astype(F32)
    RM[0, yh, c] = 0.5 * (jnp.log(mine_r) - 20.0)
    CM[x, yl] = 0.5 * jnp.log(mine_c)

    barrier = pltpu.get_barrier_semaphore()
    partners = [to_core, to_yh, to_diag, to_yl, to_xp, to_xm, to_x2] + [to_z(r) for r in rel[1:]]
    for dev in partners:
        pl.semaphore_signal(barrier, inc=1, device_id=dev, device_id_type=MESH)
    pl.semaphore_wait(barrier, len(partners))

    def send_a(r, up):
        to = place_of(r - 1 if up else r + 1)
        send(rows.at[:, place(r), yh, c], rows.at[:, to, yh, c], r_a.at[to], to_zp if up else to_zm, 2)

    def step_a(d):
        for sign in (-1, 1):
            arrive(rows.at[:, place(sign * d), yh, c], r_a.at[place(sign * d)])
            if d < H - 1 or sign < 0:
                send_a(sign * d, sign < 0)

    def send_b(s, r, up):
        to = place_of(r - 1 if up else r + 1)
        ref, dst = rows.at[s, place(r), 1 - yh, c], rows.at[s, to, 1 - yh, c]
        send(ref, dst, r_b.at[s, to], to_zp if up else to_zm, 1)

    def step_b(s, d):
        for sign in (-1, 1) if d > 0 else (1,):
            arrive(rows.at[s, place(sign * d), 1 - yh, c], r_b.at[s, place(sign * d)])
            if d == 0:
                send_b(s, 0, True)
            if d < H - 1:
                send_b(s, sign * d, sign < 0)

    def far_out():
        arrive(rows.at[:, NZ - 1, yh, c], r_a.at[NZ - 1])
        send(rows.at[:, NZ - 1, yh, c], rows.at[:, NZ - 1, yh, c], r_far, to_yh, 2)

    def far_here():
        arrive(rows.at[:, NZ - 1, 1 - yh, c], r_far)

    def row_core(s, j):
        ref = rows.at[s, pl.ds(2 * j, 2), :, c]
        send(ref, ref, r_core.at[s, j], to_core, 4)

    def core_here(s, j):
        arrive(rows.at[s, pl.ds(2 * j, 2), :, oc], r_core.at[s, j])

    def send_col(r, up):
        send(cols.at[:, r], cols.at[:, r], r_col.at[r], to_xp if up else to_xm, 2)

    def col_here(r):
        arrive(cols.at[:, r], r_col.at[r])

    def margs_out():
        me = RM.at[0, yh, c]
        for i, dev in enumerate((to_core, to_yh, to_diag)):
            send_small(me, me, s_mo.at[i], r_mo.at[i], dev)
        send_small(CM.at[x, yl], CM.at[x, yl], s_nx.at[3], r_nx.at[3], to_yl)

    def margs_x():
        arrive(CM.at[x, 1 - yl], r_nx.at[3])
        for i, dev in enumerate((to_xp, to_xm, to_x2)):
            send_small(CM.at[x], CM.at[x], s_nx.at[i], r_nx.at[i], dev)

    def margs_z():
        arrive(RM.at[0, yh, oc], r_mo.at[0])
        arrive(RM.at[0, 1 - yh, c], r_mo.at[1])
        arrive(RM.at[0, 1 - yh, oc], r_mo.at[2])
        for p in range(1, NZ):
            to = place_of(-rel[p])
            send_small(RM.at[0], RM.at[to], s_mz.at[p], r_mz.at[to], to_z(rel[p]))

    def preps(lo, hi):
        def chunk(q, carry):
            count_copy(q).wait()

            def part(i, carry):
                at = pl.ds(pl.multiple_of(i * 32, 32), 32)
                n = cnt[pl.ds(pl.multiple_of(q * 4 * B + i * 32, 32), 32), :].astype(F32)
                m = jnp.maximum(n, 1.0)
                conf = jnp.where(n > 0, 0.4 + m * lax.rsqrt(m), 0.0)
                PA[q, at, :] = conf
                PB[q, at, :] = 0.5 * conf * jnp.log(m)
                return carry

            return lax.fori_loop(0, 4 * B // 32, part, carry)

        lax.fori_loop(lo, hi, chunk, 0)

    def halves(s, a, b):
        return jnp.concatenate([a[:, s * B : (s + 1) * B], b[:, s * B : (s + 1) * B]], axis=1)

    def col_lines():
        for s in range(NS):
            for j in range(CN // 128):
                a, b = divmod(2 * j, XN), divmod(2 * j + 1, XN)
                LC[s, :, j * 128 : (j + 1) * 128] = halves(s, CM[a[1], a[0]], CM[b[1], b[0]])

    def lift(p):
        for y in range(2):
            for k in range(2):
                wide = jnp.broadcast_to(RM[p, y, k], (128, 2 * B)).T
                for s in range(NS):
                    LRB[s, p, (y * 2 + k) * B : (y * 2 + k + 1) * B, :] = wide[s * B : (s + 1) * B]

    def unit(s, p, k):
        left = rows[s, p].reshape(4 * B, D)
        lr = LRB[s, p]
        t = dot(left, colsT[s], NN) + jnp.concatenate([lr] * (CN // 128), axis=1) + LC[s]
        conf = PA[s * NZ + p]
        g = jnp.where(conf > 0, conf * t - PB[s * NZ + p], jnp.tanh(t) + 1.0).astype(BF16)
        RP[k] = dot(g, cols[s].reshape(CN, D), NN).reshape(2, 2, B, D)
        OWN[s, p] = RP[k, :, c]
        CS[s, p] = RP[k, :, oc].astype(BF16)
        return dot(left.T, g, NN)

    def sums_here(s, j):
        arrive(CR.at[s, pl.ds(2 * j, 2)], r_cr.at[s, j])

    def chip_sum(s, r):
        return OWN[s, place(r)] + CR[s, place(r)].astype(F32)

    def ring(s, d):
        if d > 0:
            sums_here(s, d - 1)
        if d == H:
            v = chip_sum(s, H)
            RSp[s, H - 1, 0] = v[0].astype(BF16)
            send(RSp.at[s, H - 1, 0], RRp.at[s, H - 1, 0], r_rp.at[s, H - 1], to_zp, 1)
            RSm[s, H - 1, 1] = v[1].astype(BF16)
            send(RSm.at[s, H - 1, 1], RRm.at[s, H - 1, 1], r_rm.at[s, H - 1], to_zm, 1)
        elif d > 0:
            for up in (True, False):
                RS, RR, rr, dev = (RSp, RRp, r_rp, to_zp) if up else (RSm, RRm, r_rm, to_zm)
                v = chip_sum(s, d if up else -d)
                if d == H - 1:
                    half = 0 if up else 1
                    arrive(RR.at[s, d, half], rr.at[s, d])
                    RS[s, d - 1, half] = (v[half] + RR[s, d, half].astype(F32)).astype(BF16)
                    RS[s, d - 1, 1 - half] = v[1 - half].astype(BF16)
                else:
                    arrive(RR.at[s, d], rr.at[s, d])
                    RS[s, d - 1] = (v + RR[s, d].astype(F32)).astype(BF16)
                send(RS.at[s, d - 1], RR.at[s, d - 1], rr.at[s, d - 1], dev, 2)
        else:
            v = chip_sum(s, 0)
            arrive(RRp.at[s, 0], r_rp.at[s, 0])
            arrive(RRm.at[s, 0], r_rm.at[s, 0])
            VR[s] = v + RRp[s, 0].astype(F32) + RRm[s, 0].astype(F32)
            YS[s] = VR[s, 1 - yh].astype(BF16)
            send(YS.at[s], YR.at[s], r_y.at[s], to_yh, 1)

    def rows_out(s):
        arrive(YR.at[s], r_y.at[s])
        nr[s] = 0.5 * (VR[s, yh] + YR[s].astype(F32))

    def col_far(s):
        CP[s] = CPT[s].T.reshape(2 * XN, B, D)
        Q1s[s, 0] = CP[s, yl * XN + x2].astype(BF16)
        send(Q1s.at[s, 0], Q1r.at[s, 0], r_q.at[s, 0], to_xp, 1)
        Q1s[s, 1] = CP[s, (1 - yl) * XN + x2].astype(BF16)
        send(Q1s.at[s, 1], Q1r.at[s, 1], r_q.at[s, 1], to_xm, 1)

    def col_near(s):
        arrive(Q1r.at[s, 0], r_q.at[s, 0])
        Q2s[s, 0, 0] = (CP[s, yl * XN + xp] + Q1r[s, 0].astype(F32)).astype(BF16)
        Q2s[s, 0, 1] = CP[s, (1 - yl) * XN + xp].astype(BF16)
        send(Q2s.at[s, 0], Q2r.at[s, 0], r_q.at[s, 2], to_xp, 2)
        arrive(Q1r.at[s, 1], r_q.at[s, 1])
        Q2s[s, 1, 0] = CP[s, yl * XN + xm].astype(BF16)
        Q2s[s, 1, 1] = (CP[s, (1 - yl) * XN + xm] + Q1r[s, 1].astype(F32)).astype(BF16)
        send(Q2s.at[s, 1], Q2r.at[s, 1], r_q.at[s, 3], to_xm, 2)

    def col_own(s):
        arrive(Q2r.at[s, 0], r_q.at[s, 2])
        arrive(Q2r.at[s, 1], r_q.at[s, 3])
        Q3s[s] = (CP[s, r_oth] + Q2r[s, 0, 1].astype(F32) + Q2r[s, 1, 1].astype(F32)).astype(BF16)
        send(Q3s.at[s], Q3r.at[s], r_q.at[s, 4], to_yl, 1)
        VC[s] = CP[s, r_own] + Q2r[s, 0, 0].astype(F32) + Q2r[s, 1, 0].astype(F32)

    def cols_out(s):
        arrive(Q3r.at[s], r_q.at[s, 4])
        nc[s] = 0.5 * (VC[s] + Q3r[s].astype(F32))

    send(rows.at[0, 0, yh, c], rows.at[0, 0, yh, c], r_b.at[0, 0], to_yh, 1)
    send_a(0, True)
    send_a(0, False)
    send(rows.at[1, 0, yh, c], rows.at[1, 0, yh, c], r_b.at[1, 0], to_yh, 1)
    send(cols.at[:, r_own], cols.at[:, r_own], r_col.at[r_own], to_yl, 2)
    send_col(r_own, True)
    send_col(r_own, False)
    margs_out()
    preps(0, 2)
    step_a(1)
    col_here(r_oth)
    send_col(r_oth, True)
    send_col(r_oth, False)
    step_b(0, 0)
    step_b(1, 0)
    margs_x()
    margs_z()
    preps(2, 5)
    step_a(2)
    col_here(yl * XN + xp)
    send_col(yl * XN + xp, False)
    col_here((1 - yl) * XN + xm)
    send_col((1 - yl) * XN + xm, True)
    step_b(0, 1)
    row_core(0, 0)
    preps(5, 8)
    step_b(1, 1)
    step_a(3)
    row_core(1, 0)
    preps(8, 11)
    for i, r in enumerate((xm, xp, x2)):
        arrive(CM.at[r], r_nx.at[i])
    col_lines()
    step_b(0, 2)
    row_core(0, 1)
    col_here((1 - yl) * XN + xp)
    col_here(yl * XN + xm)
    col_here(yl * XN + x2)
    col_here((1 - yl) * XN + x2)
    for s in range(NS):
        colsT[s] = (cols[s].reshape(CN, D).astype(F32) * 0.5).T.astype(BF16)
        CPT[s] = jnp.zeros_like(CPT[s])
    step_b(1, 2)
    row_core(1, 1)
    preps(11, 2 * NZ)

    def before(i):
        if i < H:
            for q in range(max(1, 2 * i), 2 * i + 2):
                arrive(RM.at[q], r_mz.at[q])
            core_here(0, i)
        if i == 1:
            far_out()
            step_b(0, 3)
            row_core(0, 2)
            step_b(1, 3)
            row_core(1, 2)
        if i == 2:
            far_here()
            row_core(0, 3)
            row_core(1, 3)
        if i == H:
            col_far(0)
            ring(0, H)
        if i == H + 1:
            ring(0, 3)
            ring(1, H)
        if i == H + 2:
            col_near(0)
            ring(0, 2)
            ring(1, 3)
        if i == H + 3:
            col_own(0)
            ring(0, 1)
            ring(1, 2)
        if i >= H:
            core_here(1, 2 * H - 1 - i)

    def step(i, carry):
        for k in range(2 * H):
            pl.when(i == k)(functools.partial(before, k))
        s = i // H
        j = i * (1 - s) + (2 * H - 1 - i) * s
        p = 2 * j

        @pl.when(i < H)
        def _():
            lift(p)
            lift(p + 1)

        CPT[s] += unit(s, p, 0) + unit(s, p + 1, 1)
        part = pl.ds(p, 2)
        send(CS.at[s, part], CR.at[s, part], r_cr.at[s, j], to_core, 4 * 2 * H)
        return carry

    lax.fori_loop(0, 2 * H, step, 0)
    col_far(1)
    ring(0, 0)
    ring(1, 1)
    cols_out(0)
    col_near(1)
    for copy in small:
        copy.wait_send()
    rows_out(0)
    ring(1, 0)
    col_own(1)
    rows_out(1)
    cols_out(1)
    n = total[0] * B * D * 2 // (CN * 4)
    arrive(cnt.at[pl.ds(0, n)], s_all)


def local(counts, re, ce, rm, cm, ra, ca, *, NZ, XN):
    S, B, D = re.shape
    CB = counts.shape[2]
    H = NZ // 2
    R = 2 * XN
    counts = counts.reshape(S, NZ, 4 * B, CB)
    vmem = pl.BlockSpec(memory_space=pltpu.VMEM)
    sem = pltpu.SemaphoreType.DMA
    v = pltpu.VMEM
    scratch = [
        v((S, B, D), F32),
        v((S, B, D), F32),
        v((S, B), jnp.int32),
        v((S, B), jnp.int32),
        v((S * NZ * 4 * B, CB), jnp.int32),
        v((S, NZ, 2, 2, B, D), BF16),
        v((S, R, B, D), BF16),
        v((S, D, CB), BF16),
        v((NZ, 2, 2, 1, 2 * B), F32),
        v((XN, 2, 1, 2 * B), F32),
        v((S, NZ, 4 * B, 128), F32),
        v((S, 1, CB), F32),
        v((S * NZ, 4 * B, CB), F32),
        v((S * NZ, 4 * B, CB), F32),
        v((2, 2, 2, B, D), F32),
        v((S, NZ, 2, B, D), F32),
        v((S, D, CB), F32),
        v((S, R, B, D), F32),
        v((S, NZ, 2, B, D), BF16),
        v((S, NZ, 2, B, D), BF16),
        v((S, H, 2, B, D), BF16),
        v((S, H, 2, B, D), BF16),
        v((S, H, 2, B, D), BF16),
        v((S, H, 2, B, D), BF16),
        v((S, B, D), BF16),
        v((S, B, D), BF16),
        v((S, 2, B, D), F32),
        v((S, 2, B, D), BF16),
        v((S, 2, B, D), BF16),
        v((S, 2, 2, B, D), BF16),
        v((S, 2, 2, B, D), BF16),
        v((S, B, D), BF16),
        v((S, B, D), BF16),
        v((S, B, D), F32),
        sem((4,)),
        sem((S * NZ,)),
        sem(()),
        sem((NZ,)),
        sem((S, NZ)),
        sem(()),
        sem((S, H)),
        sem((R,)),
        sem((NZ,)),
        sem((NZ,)),
        sem((3,)),
        sem((3,)),
        sem((4,)),
        sem((4,)),
        sem((S, H)),
        sem((S, H)),
        sem((S, H)),
        sem((S,)),
        sem((S, 5)),
    ]
    gr, gc = pl.pallas_call(
        functools.partial(kernel, NZ, XN, B, D, CB),
        out_shape=(jax.ShapeDtypeStruct((S, B, D), F32), jax.ShapeDtypeStruct((S, B, D), F32)),
        in_specs=[pl.BlockSpec(memory_space=pltpu.HBM)] * 5,
        out_specs=(vmem, vmem),
        scratch_shapes=scratch,
        compiler_params=pltpu.CompilerParams(
            collective_id=0, has_side_effects=True, vmem_limit_bytes=60 * 1024 * 1024
        ),
    )(counts, re, ce, rm, cm)
    return adagrad(re, ra, gr), adagrad(ce, ca, gc)


def solution(mesh):
    return jax.shard_map(
        functools.partial(local, NZ=mesh.shape["col"] // 4, XN=mesh.shape["row"] // 2),
        mesh=mesh,
        in_specs=(
            P(None, "row", "col"),
            P(None, ("row", "col"), None),
            P(None, ("col", "row"), None),
            P(None, ("row", "col")),
            P(None, ("col", "row")),
            P(None, ("row", "col"), None),
            P(None, ("col", "row"), None),
        ),
        out_specs=(P(None, ("row", "col"), None), P(None, ("col", "row"), None)),
        check_vma=False,
    )
```

time: 556 us -> 62.2 us (0.11)
  waiting for transfers between devices: 307 us -> 0 us
  blocking collectives: 199 us -> 0 us
  Pallas kernels: 0 us -> 59.6 us
  matrix products: 20.1 us -> 0 us
  between operations: 15.5 us -> 0.7 us
  local copies, waits for them, and re-layouts: 9.44 us -> 0.02 us
    reduce_scatter x4 -> x0, waiting for transfers between devices: 306 us -> none  [the longest x2 243 us: process(): lax.psum_scatter(row_terms, 'col', scatter_dimension=1, tiled=True)]
    unnamed x2 -> x0, blocking collectives: 142 us -> none
    pallas_call x0 -> x1, Pallas kernels: none -> 59.6 us  [local(): pl.pallas_call(functools.partial(kernel, NZ, XN, B, D, CB), out_shape=(ja...]
    all_gather x2 -> x0, blocking collectives: 57 us -> none  [process(): lax.all_gather(col_embed.astype(jnp.bfloat16), 'row', axis=1, tiled=True)]
    dot_general x6 -> x0, matrix products: 20.1 us -> none  [the longest x2 11.2 us: cell_grads(): jnp.einsum('srd,scd->src', rows_half, cols_half, preferred_element_type=j...]
    unnamed x24 -> x8, local copies, waits for them, and re-layouts: 7.06 us -> 0.02 us
  transfers between devices with their start and end apart: 6 -> 0, of which waited for: 4 -> 0; matrix products, arithmetic and copies ran while one was open for 5% -> 0% of each run, Pallas kernels for 0% -> 0%
where the time goes in v1:
time: 62.2 us; the launch traced here: 62.1 us
  Pallas kernels  59.6 us (96%)
  other arithmetic  1.72 us (3%)
  between operations  0.7 us (1%)
    pallas_call x1, Pallas kernels, local(): pl.pallas_call(functools.partial(kernel, NZ, XN, B, D, CB), out_shape=(ja...  59.6 us
    sub x1, other arithmetic, adagrad(): return w - g / jnp.sqrt(a + g * g)  1.72 us

profile of v1, /device:TPU:8, one launch (start us, length us, event | category | flops | bytes accessed | tf_op | source)
XLA Modules:
  0.0 62.1 jit_solution(4610144009527001665)
XLA Ops:
  0.6 0.0 copy-start
  0.6 0.0 copy-start.1
  0.7 0.0 copy-start.2
  0.7 0.0 copy-start.3
  0.7 59.6 %shard_map.86 = (f32[2,64,256]{2,1,0:T(8,128)}, f32[2,64,256]{2,1,0:T(8,128)}) custom-call(s32[2,8,256,512]{3,2,1,0:T(8,128)} %bitcast.1, f32[2,64,256]{2,1,0:T(8,128)} %re_h.1, f32[2,64,256]{2,1,0:T(8,128)} %ce_h.1, s32[2,64]{1,0:T(2,128)} %rm_h.1, s32[2,64]{1,0:T(2,128)} %cm_h.1), custom_call_target="tpu_custom_call" | custom-call | tf_op jit(solution)/shard_map/pallas_call | solution.py:479
  60.3 0.0 copy-done
  60.3 0.0 copy-done.1
  60.3 0.0 copy-done.2
  60.3 0.0 copy-done.3
  60.3 1.7 %multiply_subtract_fusion = (f32[2,64,256]{2,1,0:T(8,128)}, f32[2,64,256]{2,1,0:T(8,128)}) fusion(f32[2,64,256]{2,1,0:T(8,128)S(1)} %copy-done, f32[2,64,256]{2,1,0:T(8,128)} %get-tuple-element.5, f32[2,64,256]{2,1,0:T(8,128)S(1)} %copy-done.2, f32[2,64,256]{2,1,0:T(8,128)S(1)} %copy-done.1, f32[2,64,256]{2,1,0:T(8,128)} %get-tuple-element.4, ...), kind=kLoop, calls=%fused_computation | loop fusion | flops 262144 | bytes 1048576 | tf_op jit(solution)/shard_map/sub | solution.py:23
Async XLA Ops:
  0.6 59.7 %copy-start = (f32[2,64,256]{2,1,0:T(8,128)S(1)}, f32[2,64,256]{2,1,0:T(8,128)}, u32[]{:S(2)}) copy-start(f32[2,64,256]{2,1,0:T(8,128)} %ce_h.1) | copy-start | bytes 393220
  0.6 59.7 %copy-start.1 = (f32[2,64,256]{2,1,0:T(8,128)S(1)}, f32[2,64,256]{2,1,0:T(8,128)}, u32[]{:S(2)}) copy-start(f32[2,64,256]{2,1,0:T(8,128)} %re_h.1) | copy-start | bytes 393220
  0.7 59.7 %copy-start.2 = (f32[2,64,256]{2,1,0:T(8,128)S(1)}, f32[2,64,256]{2,1,0:T(8,128)}, u32[]{:S(2)}) copy-start(f32[2,64,256]{2,1,0:T(8,128)} %param.13) | copy-start | bytes 393220
  0.7 59.7 %copy-start.3 = (f32[2,64,256]{2,1,0:T(8,128)S(1)}, f32[2,64,256]{2,1,0:T(8,128)}, u32[]{:S(2)}) copy-start(f32[2,64,256]{2,1,0:T(8,128)} %param.12) | copy-start | bytes 393220

commit v2 on v1

--- a/solution.py
+++ b/solution.py
@@ -28,8 +28,8 @@
     counts, re_h, ce_h, rm_h, cm_h, nr, nc,
     re, ce, rm, cm,
     cnt, rows, cols, colsT, RM, CM, LRB, LC, PA, PB, RP, OWN, CPT, CP,
-    CS, CR, RSp, RSm, RRp, RRm, YS, YR, VR, Q1s, Q1r, Q2s, Q2r, Q3s, Q3r, VC,
-    s_in, s_cnt, s_all, r_a, r_b, r_far, r_core, r_col, r_mz, s_mz, r_mo, s_mo, r_nx, s_nx, r_cr, r_rp, r_rm, r_y, r_q,
+    CS, CR, RSp, RSm, RRp, RRm, YS, YR, VR, Q1s, Q1r, Q2s, Q2r, Q3s, Q3r, VC, gr, gc,
+    s_in, s_cnt, s_all, s_out, r_row, r_core, r_col, r_mz, s_mz, r_mo, s_mo, r_nx, s_nx, r_cr, r_rp, r_rm, r_y, r_q,
 ):
     H = NZ // 2
     NS = 2
@@ -101,14 +101,21 @@
     for copy in own_in:
         copy.start()
 
-    def count_copy(q, r=0):
-        zc = lax.rem(z + r + NZ, NZ)
-        at = pl.ds(q * 4 * B, 4 * B)
+    barrier = pltpu.get_barrier_semaphore()
+    partners = [to_core, to_yh, to_diag, to_yl, to_xp, to_xm, to_x2] + [to_z(r) for r in rel[1:]]
+    for dev in partners:
+        pl.semaphore_signal(barrier, inc=1, device_id=dev, device_id_type=MESH)
+
+    def count_copy(q):
+        p = lax.rem(q, NZ)
+        d = (p + 1) // 2
+        zc = lax.rem(z + NZ + d * (2 * lax.rem(p, 2) - 1), NZ)
+        at = pl.ds(pl.multiple_of(q * 4 * B, 4 * B), 4 * B)
         return pltpu.make_async_copy(counts.at[q // NZ, zc], cnt.at[at], s_cnt.at[q])
 
-    for s in range(NS):
-        for p in range(NZ):
-            count_copy(s * NZ + p, rel[p]).start()
+    AHEAD = 3
+    for q in range(AHEAD):
+        count_copy(q).start()
 
     for copy in own_in:
         copy.wait()
@@ -120,41 +127,36 @@
     RM[0, yh, c] = 0.5 * (jnp.log(mine_r) - 20.0)
     CM[x, yl] = 0.5 * jnp.log(mine_c)
 
-    barrier = pltpu.get_barrier_semaphore()
-    partners = [to_core, to_yh, to_diag, to_yl, to_xp, to_xm, to_x2] + [to_z(r) for r in rel[1:]]
-    for dev in partners:
-        pl.semaphore_signal(barrier, inc=1, device_id=dev, device_id_type=MESH)
     pl.semaphore_wait(barrier, len(partners))
 
-    def send_a(r, up):
+    def row_block(s, p, y):
+        return rows.at[s, p, 1 - yh if y else yh, c]
+
+    def send_row(s, y, r, up):
         to = place_of(r - 1 if up else r + 1)
-        send(rows.at[:, place(r), yh, c], rows.at[:, to, yh, c], r_a.at[to], to_zp if up else to_zm, 2)
-
-    def step_a(d):
+        send(row_block(s, place(r), y), row_block(s, to, y), r_row.at[s, to, y], to_zp if up else to_zm, 1)
+
+    def row_here(s, y, r):
+        arrive(row_block(s, place_of(r), y), r_row.at[s, place_of(r), y])
+
+    def row_step(s, y, d):
         for sign in (-1, 1):
-            arrive(rows.at[:, place(sign * d), yh, c], r_a.at[place(sign * d)])
-            if d < H - 1 or sign < 0:
-                send_a(sign * d, sign < 0)
-
-    def send_b(s, r, up):
-        to = place_of(r - 1 if up else r + 1)
-        ref, dst = rows.at[s, place(r), 1 - yh, c], rows.at[s, to, 1 - yh, c]
-        send(ref, dst, r_b.at[s, to], to_zp if up else to_zm, 1)
-
-    def step_b(s, d):
-        for sign in (-1, 1) if d > 0 else (1,):
-            arrive(rows.at[s, place(sign * d), 1 - yh, c], r_b.at[s, place(sign * d)])
-            if d == 0:
-                send_b(s, 0, True)
-            if d < H - 1:
-                send_b(s, sign * d, sign < 0)
-
-    def far_out():
-        arrive(rows.at[:, NZ - 1, yh, c], r_a.at[NZ - 1])
-        send(rows.at[:, NZ - 1, yh, c], rows.at[:, NZ - 1, yh, c], r_far, to_yh, 2)
-
-    def far_here():
-        arrive(rows.at[:, NZ - 1, 1 - yh, c], r_far)
+            row_here(s, y, sign * d)
+            if d < H - 1 or (y == 0 and sign < 0):
+                send_row(s, y, sign * d, sign < 0)
+
+    def row_y(s):
+        row_here(s, 1, 0)
+        send_row(s, 1, 0, True)
+        send_row(s, 1, 0, False)
+
+    def far_out(s):
+        row_here(s, 0, H)
+        ref = row_block(s, NZ - 1, 0)
+        send(ref, ref, r_row.at[s, NZ - 1, 1], to_yh, 1)
+
+    def far_here(s):
+        row_here(s, 1, H)
 
     def row_core(s, j):
         ref = rows.at[s, pl.ds(2 * j, 2), :, c]
@@ -190,6 +192,14 @@
 
     def preps(lo, hi):
         def chunk(q, carry):
+            @pl.when(q < NZ)
+            def _():
+                count_copy(q + NZ).start()
+
+            @pl.when(q + AHEAD < NZ)
+            def _():
+                count_copy(q + AHEAD).start()
+
             count_copy(q).wait()
 
             def part(i, carry):
@@ -214,12 +224,14 @@
                 a, b = divmod(2 * j, XN), divmod(2 * j + 1, XN)
                 LC[s, :, j * 128 : (j + 1) * 128] = halves(s, CM[a[1], a[0]], CM[b[1], b[0]])
 
-    def lift(p):
-        for y in range(2):
-            for k in range(2):
-                wide = jnp.broadcast_to(RM[p, y, k], (128, 2 * B)).T
-                for s in range(NS):
-                    LRB[s, p, (y * 2 + k) * B : (y * 2 + k + 1) * B, :] = wide[s * B : (s + 1) * B]
+    def lift():
+        lines = [RM[p, y, k] for p in range(NZ) for y in range(2) for k in range(2)]
+        wide = jnp.concatenate(lines, axis=0).T
+        for i in range(4 * NZ):
+            p, b = divmod(i, 4)
+            for s in range(NS):
+                column = wide[s * B : (s + 1) * B, i : i + 1]
+                LRB[s, p, b * B : (b + 1) * B, :] = jnp.broadcast_to(column, (B, 128))
 
     def unit(s, p, k):
         left = rows[s, p].reshape(4 * B, D)
@@ -268,9 +280,14 @@
             YS[s] = VR[s, 1 - yh].astype(BF16)
             send(YS.at[s], YR.at[s], r_y.at[s], to_yh, 1)
 
+    def out_copy(k, s):
+        src, dst = ((gr, nr), (gc, nc))[k]
+        return pltpu.make_async_copy(src.at[s], dst.at[s], s_out.at[k, s])
+
     def rows_out(s):
         arrive(YR.at[s], r_y.at[s])
-        nr[s] = 0.5 * (VR[s, yh] + YR[s].astype(F32))
+        gr[s] = 0.5 * (VR[s, yh] + YR[s].astype(F32))
+        out_copy(0, s).start()
 
     def col_far(s):
         CP[s] = CPT[s].T.reshape(2 * XN, B, D)
@@ -298,69 +315,87 @@
 
     def cols_out(s):
         arrive(Q3r.at[s], r_q.at[s, 4])
-        nc[s] = 0.5 * (VC[s] + Q3r[s].astype(F32))
-
-    send(rows.at[0, 0, yh, c], rows.at[0, 0, yh, c], r_b.at[0, 0], to_yh, 1)
-    send_a(0, True)
-    send_a(0, False)
-    send(rows.at[1, 0, yh, c], rows.at[1, 0, yh, c], r_b.at[1, 0], to_yh, 1)
-    send(cols.at[:, r_own], cols.at[:, r_own], r_col.at[r_own], to_yl, 2)
-    send_col(r_own, True)
-    send_col(r_own, False)
-    margs_out()
-    preps(0, 2)
-    step_a(1)
+        gc[s] = 0.5 * (VC[s] + Q3r[s].astype(F32))
+        out_copy(1, s).start()
+
+    for s in range(NS):
+        send(row_block(s, 0, 0), row_block(s, 0, 0), r_row.at[s, 0, 1], to_yh, 1)
+        send_row(s, 0, 0, True)
+        send_row(s, 0, 0, False)
+        if s == 0:
+            send(cols.at[:, r_own], cols.at[:, r_own], r_col.at[r_own], to_yl, 2)
+            send_col(r_own, True)
+            send_col(r_own, False)
+            margs_out()
+    preps(0, 1)
+    row_step(0, 0, 1)
     col_here(r_oth)
     send_col(r_oth, True)
     send_col(r_oth, False)
-    step_b(0, 0)
-    step_b(1, 0)
+    row_step(1, 0, 1)
+    row_y(0)
     margs_x()
+    preps(1, 2)
+    row_step(0, 0, 2)
+    row_y(1)
     margs_z()
-    preps(2, 5)
-    step_a(2)
+    row_step(1, 0, 2)
     col_here(yl * XN + xp)
     send_col(yl * XN + xp, False)
     col_here((1 - yl) * XN + xm)
     send_col((1 - yl) * XN + xm, True)
-    step_b(0, 1)
+    preps(2, 4)
+    row_step(0, 1, 1)
     row_core(0, 0)
-    preps(5, 8)
-    step_b(1, 1)
-    step_a(3)
+    row_step(0, 0, 3)
+    preps(4, 5)
+    row_step(1, 0, 3)
+    row_step(1, 1, 1)
     row_core(1, 0)
-    preps(8, 11)
+    preps(5, 7)
+    row_step(0, 1, 2)
+    row_core(0, 1)
+    far_out(0)
+    preps(7, 8)
+    for p in range(1, NZ):
+        arrive(RM.at[p], r_mz.at[p])
+    lift()
     for i, r in enumerate((xm, xp, x2)):
         arrive(CM.at[r], r_nx.at[i])
     col_lines()
-    step_b(0, 2)
-    row_core(0, 1)
+    row_step(1, 1, 2)
+    row_core(1, 1)
     col_here((1 - yl) * XN + xp)
     col_here(yl * XN + xm)
     col_here(yl * XN + x2)
     col_here((1 - yl) * XN + x2)
-    for s in range(NS):
-        colsT[s] = (cols[s].reshape(CN, D).astype(F32) * 0.5).T.astype(BF16)
+
+    def turn(s):
+        colsT[s] = (cols[s].reshape(CN, D) * 0.5).T
         CPT[s] = jnp.zeros_like(CPT[s])
-    step_b(1, 2)
-    row_core(1, 1)
-    preps(11, 2 * NZ)
+
+    turn(0)
 
     def before(i):
         if i < H:
-            for q in range(max(1, 2 * i), 2 * i + 2):
-                arrive(RM.at[q], r_mz.at[q])
+            if i == 1:
+                row_step(0, 1, 3)
+                row_core(0, 2)
+                far_out(1)
+            if i == 2:
+                far_here(0)
+                row_core(0, 3)
+                row_step(1, 1, 3)
+                row_core(1, 2)
+            if i == 3:
+                far_here(1)
+                row_core(1, 3)
             core_here(0, i)
-        if i == 1:
-            far_out()
-            step_b(0, 3)
-            row_core(0, 2)
-            step_b(1, 3)
-            row_core(1, 2)
-        if i == 2:
-            far_here()
-            row_core(0, 3)
-            row_core(1, 3)
+            return
+        if i == H:
+            turn(1)
+        preps(2 * NZ - 2 * (i - H) - 2, 2 * NZ - 2 * (i - H))
+        core_here(1, 2 * H - 1 - i)
         if i == H:
             col_far(0)
             ring(0, H)
@@ -375,8 +410,6 @@
             col_own(0)
             ring(0, 1)
             ring(1, 2)
-        if i >= H:
-            core_here(1, 2 * H - 1 - i)
 
     def step(i, carry):
         for k in range(2 * H):
@@ -384,12 +417,6 @@
         s = i // H
         j = i * (1 - s) + (2 * H - 1 - i) * s
         p = 2 * j
-
-        @pl.when(i < H)
-        def _():
-            lift(p)
-            lift(p + 1)
-
         CPT[s] += unit(s, p, 0) + unit(s, p + 1, 1)
         part = pl.ds(p, 2)
         send(CS.at[s, part], CR.at[s, part], r_cr.at[s, j], to_core, 4 * 2 * H)
@@ -406,8 +433,11 @@
     rows_out(0)
     ring(1, 0)
     col_own(1)
+    cols_out(1)
     rows_out(1)
-    cols_out(1)
+    for k in range(2):
+        for s in range(NS):
+            out_copy(k, s).wait()
     n = total[0] * B * D * 2 // (CN * 4)
     arrive(cnt.at[pl.ds(0, n)], s_all)
 
@@ -418,7 +448,6 @@
     H = NZ // 2
     R = 2 * XN
     counts = counts.reshape(S, NZ, 4 * B, CB)
-    vmem = pl.BlockSpec(memory_space=pltpu.VMEM)
     sem = pltpu.SemaphoreType.DMA
     v = pltpu.VMEM
     scratch = [
@@ -456,12 +485,13 @@
         v((S, B, D), BF16),
         v((S, B, D), BF16),
         v((S, B, D), F32),
+        v((S, B, D), F32),
+        v((S, B, D), F32),
         sem((4,)),
         sem((S * NZ,)),
         sem(()),
-        sem((NZ,)),
-        sem((S, NZ)),
-        sem(()),
+        sem((2, S)),
+        sem((S, NZ, 2)),
         sem((S, H)),
         sem((R,)),
         sem((NZ,)),
@@ -480,7 +510,7 @@
         functools.partial(kernel, NZ, XN, B, D, CB),
         out_shape=(jax.ShapeDtypeStruct((S, B, D), F32), jax.ShapeDtypeStruct((S, B, D), F32)),
         in_specs=[pl.BlockSpec(memory_space=pltpu.HBM)] * 5,
-        out_specs=(vmem, vmem),
+        out_specs=(pl.BlockSpec(memory_space=pltpu.HBM),) * 2,
         scratch_shapes=scratch,
         compiler_params=pltpu.CompilerParams(
             collective_id=0, has_side_effects=True, vmem_limit_bytes=60 * 1024 * 1024

time: 62.2 us -> 57.7 us (0.928)
  Pallas kernels: 59.6 us -> 55.2 us
    pallas_call x1, Pallas kernels: 59.6 us -> 55.2 us  [local(): pl.pallas_call(functools.partial(kernel, NZ, XN, B, D, CB), out_shape=(ja...]
where the time goes in v2:
time: 57.7 us; the launch traced here: 57.6 us
  Pallas kernels  55.2 us (96%)
  other arithmetic  1.72 us (3%)
  between operations  0.7 us (1%)
    pallas_call x1, Pallas kernels, local(): pl.pallas_call(functools.partial(kernel, NZ, XN, B, D, CB), out_shape=(ja...  55.2 us
    sub x1, other arithmetic, adagrad(): return w - g / jnp.sqrt(a + g * g)  1.72 us

profile of v2, /device:TPU:8, one launch (start us, length us, event | category | flops | bytes accessed | tf_op | source)
XLA Modules:
  0.0 57.6 jit_solution(6770412573299981203)
XLA Ops:
  0.6 0.0 copy-start
  0.6 0.0 copy-start.1
  0.7 0.0 copy-start.2
  0.7 0.0 copy-start.3
  0.7 55.2 %shard_map.86 = (f32[2,64,256]{2,1,0:T(8,128)}, f32[2,64,256]{2,1,0:T(8,128)}) custom-call(s32[2,8,256,512]{3,2,1,0:T(8,128)} %bitcast.1, f32[2,64,256]{2,1,0:T(8,128)} %re_h.1, f32[2,64,256]{2,1,0:T(8,128)} %ce_h.1, s32[2,64]{1,0:T(2,128)} %rm_h.1, s32[2,64]{1,0:T(2,128)} %cm_h.1), custom_call_target="tpu_custom_call" | custom-call | tf_op jit(solution)/shard_map/pallas_call | solution.py:509
  55.8 0.0 copy-done
  55.8 0.0 copy-done.1
  55.9 0.0 copy-done.2
  55.9 0.0 copy-done.3
  55.9 1.7 %multiply_subtract_fusion = (f32[2,64,256]{2,1,0:T(8,128)}, f32[2,64,256]{2,1,0:T(8,128)}) fusion(f32[2,64,256]{2,1,0:T(8,128)S(1)} %copy-done, f32[2,64,256]{2,1,0:T(8,128)} %get-tuple-element.5, f32[2,64,256]{2,1,0:T(8,128)S(1)} %copy-done.2, f32[2,64,256]{2,1,0:T(8,128)S(1)} %copy-done.1, f32[2,64,256]{2,1,0:T(8,128)} %get-tuple-element.4, ...), kind=kLoop, calls=%fused_computation | loop fusion | flops 262144 | bytes 1048576 | tf_op jit(solution)/shard_map/sub | solution.py:23
Async XLA Ops:
  0.6 55.2 %copy-start = (f32[2,64,256]{2,1,0:T(8,128)S(1)}, f32[2,64,256]{2,1,0:T(8,128)}, u32[]{:S(2)}) copy-start(f32[2,64,256]{2,1,0:T(8,128)} %ce_h.1) | copy-start | bytes 393220
  0.6 55.2 %copy-start.1 = (f32[2,64,256]{2,1,0:T(8,128)S(1)}, f32[2,64,256]{2,1,0:T(8,128)}, u32[]{:S(2)}) copy-start(f32[2,64,256]{2,1,0:T(8,128)} %re_h.1) | copy-start | bytes 393220
  0.7 55.2 %copy-start.2 = (f32[2,64,256]{2,1,0:T(8,128)S(1)}, f32[2,64,256]{2,1,0:T(8,128)}, u32[]{:S(2)}) copy-start(f32[2,64,256]{2,1,0:T(8,128)} %param.13) | copy-start | bytes 393220
  0.7 55.2 %copy-start.3 = (f32[2,64,256]{2,1,0:T(8,128)S(1)}, f32[2,64,256]{2,1,0:T(8,128)}, u32[]{:S(2)}) copy-start(f32[2,64,256]{2,1,0:T(8,128)} %param.12) | copy-start | bytes 393220

commit v3 on v2

--- a/solution.py
+++ b/solution.py
@@ -106,7 +106,11 @@
     for dev in partners:
         pl.semaphore_signal(barrier, inc=1, device_id=dev, device_id_type=MESH)
 
-    def count_copy(q):
+    def in_turn(u):
+        return lax.rem(u // 2, 2) * NZ + u // 4 * 2 + lax.rem(u, 2)
+
+    def count_copy(u):
+        q = in_turn(u)
         p = lax.rem(q, NZ)
         d = (p + 1) // 2
         zc = lax.rem(z + NZ + d * (2 * lax.rem(p, 2) - 1), NZ)
@@ -114,8 +118,8 @@
         return pltpu.make_async_copy(counts.at[q // NZ, zc], cnt.at[at], s_cnt.at[q])
 
     AHEAD = 3
-    for q in range(AHEAD):
-        count_copy(q).start()
+    for u in range(AHEAD):
+        count_copy(u).start()
 
     for copy in own_in:
         copy.wait()
@@ -191,16 +195,13 @@
             send_small(RM.at[0], RM.at[to], s_mz.at[p], r_mz.at[to], to_z(rel[p]))
 
     def preps(lo, hi):
-        def chunk(q, carry):
-            @pl.when(q < NZ)
+        def chunk(u, carry):
+            @pl.when(u + AHEAD < NS * NZ)
             def _():
-                count_copy(q + NZ).start()
-
-            @pl.when(q + AHEAD < NZ)
-            def _():
-                count_copy(q + AHEAD).start()
-
-            count_copy(q).wait()
+                count_copy(u + AHEAD).start()
+
+            count_copy(u).wait()
+            q = in_turn(u)
 
             def part(i, carry):
                 at = pl.ds(pl.multiple_of(i * 32, 32), 32)
@@ -352,11 +353,11 @@
     row_step(1, 0, 3)
     row_step(1, 1, 1)
     row_core(1, 0)
-    preps(5, 7)
+    preps(5, 8)
     row_step(0, 1, 2)
     row_core(0, 1)
     far_out(0)
-    preps(7, 8)
+    preps(8, 10)
     for p in range(1, NZ):
         arrive(RM.at[p], r_mz.at[p])
     lift()
@@ -375,47 +376,33 @@
         CPT[s] = jnp.zeros_like(CPT[s])
 
     turn(0)
+    turn(1)
 
     def before(i):
-        if i < H:
-            if i == 1:
-                row_step(0, 1, 3)
-                row_core(0, 2)
-                far_out(1)
-            if i == 2:
-                far_here(0)
-                row_core(0, 3)
-                row_step(1, 1, 3)
-                row_core(1, 2)
-            if i == 3:
-                far_here(1)
-                row_core(1, 3)
-            core_here(0, i)
-            return
-        if i == H:
-            turn(1)
-        preps(2 * NZ - 2 * (i - H) - 2, 2 * NZ - 2 * (i - H))
-        core_here(1, 2 * H - 1 - i)
-        if i == H:
-            col_far(0)
-            ring(0, H)
-        if i == H + 1:
-            ring(0, 3)
-            ring(1, H)
-        if i == H + 2:
-            col_near(0)
-            ring(0, 2)
-            ring(1, 3)
-        if i == H + 3:
-            col_own(0)
-            ring(0, 1)
-            ring(1, 2)
+        if i == 1:
+            row_step(0, 1, 3)
+            row_core(0, 2)
+            far_out(1)
+        if i == 2:
+            preps(10, 12)
+        if i == 3:
+            far_here(0)
+            row_core(0, 3)
+            row_step(1, 1, 3)
+            row_core(1, 2)
+            preps(12, 14)
+        if i == 4:
+            far_here(1)
+            row_core(1, 3)
+        if i == 5:
+            preps(14, 16)
+        core_here(i % 2, i // 2)
 
     def step(i, carry):
         for k in range(2 * H):
             pl.when(i == k)(functools.partial(before, k))
-        s = i // H
-        j = i * (1 - s) + (2 * H - 1 - i) * s
+        s = lax.rem(i, 2)
+        j = i // 2
         p = 2 * j
         CPT[s] += unit(s, p, 0) + unit(s, p + 1, 1)
         part = pl.ds(p, 2)
@@ -423,17 +410,27 @@
         return carry
 
     lax.fori_loop(0, 2 * H, step, 0)
+    ring(0, H)
+    col_far(0)
+    ring(1, H)
     col_far(1)
-    ring(0, 0)
+    ring(0, 3)
+    ring(1, 3)
+    col_near(0)
+    col_near(1)
+    ring(0, 2)
+    ring(1, 2)
+    col_own(0)
+    col_own(1)
+    ring(0, 1)
     ring(1, 1)
     cols_out(0)
-    col_near(1)
+    cols_out(1)
     for copy in small:
         copy.wait_send()
+    ring(0, 0)
+    ring(1, 0)
     rows_out(0)
-    ring(1, 0)
-    col_own(1)
-    cols_out(1)
     rows_out(1)
     for k in range(2):
         for s in range(NS):

time: 57.7 us -> 58.1 us (level)
  the two profiles are of different devices: /device:TPU:8 before, /device:TPU:32 now
where the time goes in v3:
time: 58.1 us; the launch traced here: 58 us
  Pallas kernels  55.5 us (96%)
  other arithmetic  1.72 us (3%)
  between operations  0.7 us (1%)
    pallas_call x1, Pallas kernels, local(): pl.pallas_call(functools.partial(kernel, NZ, XN, B, D, CB), out_shape=(ja...  55.5 us
    sub x1, other arithmetic, adagrad(): return w - g / jnp.sqrt(a + g * g)  1.72 us

profile of v3, /device:TPU:32, one launch (start us, length us, event | category | flops | bytes accessed | tf_op | source)
XLA Modules:
  0.0 58.0 jit_solution(15256314027823332472)
XLA Ops:
  0.6 0.0 copy-start
  0.6 0.0 copy-start.1
  0.7 0.0 copy-start.2
  0.7 0.0 copy-start.3
  0.7 55.5 %shard_map.86 = (f32[2,64,256]{2,1,0:T(8,128)}, f32[2,64,256]{2,1,0:T(8,128)}) custom-call(s32[2,8,256,512]{3,2,1,0:T(8,128)} %bitcast.1, f32[2,64,256]{2,1,0:T(8,128)} %re_h.1, f32[2,64,256]{2,1,0:T(8,128)} %ce_h.1, s32[2,64]{1,0:T(2,128)} %rm_h.1, s32[2,64]{1,0:T(2,128)} %cm_h.1), custom_call_target="tpu_custom_call" | custom-call | tf_op jit(solution)/shard_map/pallas_call | solution.py:506
  56.2 0.0 copy-done
  56.2 0.0 copy-done.1
  56.2 0.0 copy-done.2
  56.2 0.0 copy-done.3
  56.2 1.7 %multiply_subtract_fusion = (f32[2,64,256]{2,1,0:T(8,128)}, f32[2,64,256]{2,1,0:T(8,128)}) fusion(f32[2,64,256]{2,1,0:T(8,128)S(1)} %copy-done, f32[2,64,256]{2,1,0:T(8,128)} %get-tuple-element.5, f32[2,64,256]{2,1,0:T(8,128)S(1)} %copy-done.2, f32[2,64,256]{2,1,0:T(8,128)S(1)} %copy-done.1, f32[2,64,256]{2,1,0:T(8,128)} %get-tuple-element.4, ...), kind=kLoop, calls=%fused_computation | loop fusion | flops 262144 | bytes 1048576 | tf_op jit(solution)/shard_map/sub | solution.py:23
Async XLA Ops:
  0.6 55.6 %copy-start = (f32[2,64,256]{2,1,0:T(8,128)S(1)}, f32[2,64,256]{2,1,0:T(8,128)}, u32[]{:S(2)}) copy-start(f32[2,64,256]{2,1,0:T(8,128)} %ce_h.1) | copy-start | bytes 393220
  0.6 55.6 %copy-start.1 = (f32[2,64,256]{2,1,0:T(8,128)S(1)}, f32[2,64,256]{2,1,0:T(8,128)}, u32[]{:S(2)}) copy-start(f32[2,64,256]{2,1,0:T(8,128)} %re_h.1) | copy-start | bytes 393220
  0.7 55.6 %copy-start.2 = (f32[2,64,256]{2,1,0:T(8,128)S(1)}, f32[2,64,256]{2,1,0:T(8,128)}, u32[]{:S(2)}) copy-start(f32[2,64,256]{2,1,0:T(8,128)} %param.13) | copy-start | bytes 393220
  0.7 55.6 %copy-start.3 = (f32[2,64,256]{2,1,0:T(8,128)S(1)}, f32[2,64,256]{2,1,0:T(8,128)}, u32[]{:S(2)}) copy-start(f32[2,64,256]{2,1,0:T(8,128)} %param.12) | copy-start | bytes 393220

commit v4 on v3

v4 whole, which is shorter than its diff:
```python
import functools

import jax
import jax.numpy as jnp
from jax import lax
from jax.experimental import pallas as pl
from jax.experimental.pallas import tpu as pltpu
from jax.sharding import PartitionSpec as P

MESH = pl.DeviceIdType.MESH
F32 = jnp.float32
BF16 = jnp.bfloat16
NT = (((1,), (1,)), ((), ()))
NN = (((1,), (0,)), ((), ()))
TN = (((0,), (0,)), ((), ()))


def dot(a, b, dims):
    return lax.dot_general(a, b, dims, preferred_element_type=F32)


def adagrad(w, a, g):
    return w - g / jnp.sqrt(a + g * g)


def kernel(
    NZ, XN, B, D, CN,
    counts, re_h, ce_h, rm_h, cm_h, nr, nc,
    re, ce, rm, cm,
    cnt, rows, cols, colsT, colsC, LRB, LC, PA, PB, RP, OWN, CPT, CP,
    CS, CR, RSp, RSm, RRp, RRm, YS, YR, VR, Q1s, Q1r, Q2s, Q2r, Q3s, Q3r, VC, gr, gc,
    s_in, s_cnt, s_all, s_out, r_row, r_core, r_col, r_cr, r_rp, r_rm, r_y, r_q,
):
    H = NZ // 2
    NS = 2
    row = lax.axis_index("row")
    col = lax.axis_index("col")
    x = lax.rem(row, XN)
    yl = row // XN
    z = col // 4
    yh = lax.rem(col // 2, 2)
    c = lax.rem(col, 2)
    oc = 1 - c
    xp = lax.rem(x + 1, XN)
    xm = lax.rem(x + XN - 1, XN)
    x2 = lax.rem(x + 2, XN)
    zp = lax.rem(z + 1, NZ)
    zm = lax.rem(z + NZ - 1, NZ)
    to_core = (row, col + 1 - 2 * c)
    to_yh = (row, col + 2 - 4 * yh)
    to_zp = (row, zp * 4 + yh * 2 + c)
    to_zm = (row, zm * 4 + yh * 2 + c)
    to_yl = ((1 - yl) * XN + x, col)
    to_xp = (yl * XN + xp, col)
    to_xm = (yl * XN + xm, col)
    r_own = yl * XN + x
    r_oth = (1 - yl) * XN + x

    def place(r):
        return 0 if r == 0 else 2 * r - 1 if r > 0 or r == -H else -2 * r

    def place_of(r):
        return place(H) if r == -H else place(r)

    def span(d):
        return (2 * d - 1, 2) if 0 < d < H else (place_of(d), 1)

    rel = [0]
    for d in range(1, H):
        rel += [d, -d]
    rel += [H]

    total = [0]
    summed = [0]

    def send(src, dst, rsem, dev, blocks, sums=0):
        pltpu.make_async_remote_copy(
            src_ref=src, dst_ref=dst, send_sem=s_all, recv_sem=rsem, device_id=dev, device_id_type=MESH
        ).start()
        total[0] += blocks
        summed[0] += sums

    def arrive(dst, rsem):
        pltpu.make_async_copy(dst, dst, rsem).wait()

    own_in = [
        pltpu.make_async_copy(src, dst, s_in.at[i])
        for i, (src, dst) in enumerate(((rm_h, rm), (cm_h, cm), (re_h, re), (ce_h, ce)))
    ]
    for copy in own_in:
        copy.start()

    barrier = pltpu.get_barrier_semaphore()
    partners = [to_core, to_yh, to_zp, to_zm, to_yl, to_xp, to_xm]
    for dev in partners:
        pl.semaphore_signal(barrier, inc=1, device_id=dev, device_id_type=MESH)

    def in_turn(u):
        return lax.rem(u // 2, 2) * NZ + u // 4 * 2 + lax.rem(u, 2)

    def count_copy(u):
        q = in_turn(u)
        p = lax.rem(q, NZ)
        d = (p + 1) // 2
        zc = lax.rem(z + NZ + d * (2 * lax.rem(p, 2) - 1), NZ)
        at = pl.ds(pl.multiple_of(q * 4 * B, 4 * B), 4 * B)
        return pltpu.make_async_copy(counts.at[q // NZ, zc], cnt.at[at], s_cnt.at[q])

    AHEAD = 3
    for u in range(AHEAD):
        count_copy(u).start()

    for copy in own_in:
        copy.wait()

    def own_block(embed, margs, shift):
        line = jnp.concatenate([margs[0:1, :], margs[1:2, :]], axis=1).astype(F32)
        line = 0.5 * (jnp.log(line) - shift)
        hi = line.astype(BF16).astype(F32)
        mid = (line - hi).astype(BF16).astype(F32)
        upper = jnp.concatenate([hi, mid], axis=1)
        lower = jnp.concatenate([line - hi - mid, jnp.zeros_like(line)], axis=1)
        which = lax.broadcasted_iota(jnp.int32, (16, 4 * B), 0)
        tail = jnp.where(which == 0, upper, jnp.where(which == 1, lower, 0.0)).astype(BF16)
        return embed[0].astype(BF16), embed[1].astype(BF16), tail

    for ref, parts in ((rows.at[0, yh, c], own_block(re, rm, 20.0)), (cols.at[r_own], own_block(ce, cm, 0.0))):
        ref[0:B] = parts[0]
        ref[B : 2 * B] = parts[1]
        ref[2 * B :] = parts[2]

    def line_of(tail):
        tail = tail.astype(F32)
        return tail[0:1, : 2 * B] + tail[0:1, 2 * B :] + tail[1:2, : 2 * B]

    pl.semaphore_wait(barrier, len(partners))

    def row_block(p, y):
        return rows.at[p, 1 - yh if y else yh, c]

    def send_row(y, r, up):
        to = place_of(r - 1 if up else r + 1)
        send(row_block(place(r), y), row_block(to, y), r_row.at[to, y], to_zp if up else to_zm, 1)

    def row_here(y, r):
        arrive(row_block(place_of(r), y), r_row.at[place_of(r), y])

    def row_step(y, d):
        for sign in (-1, 1):
            row_here(y, sign * d)
            if d < H - 1 or (y == 0 and sign < 0):
                send_row(y, sign * d, sign < 0)

    def far_out():
        row_here(0, H)
        send(row_block(NZ - 1, 0), row_block(NZ - 1, 0), r_row.at[NZ - 1, 1], to_yh, 1)

    def row_core(j):
        ref = rows.at[pl.ds(2 * j, 2), :, c]
        send(ref, ref, r_core.at[j], to_core, 4)

    def core_here(j):
        arrive(rows.at[pl.ds(2 * j, 2), :, oc], r_core.at[j])

    def send_col(r, up):
        send(cols.at[r], cols.at[r], r_col.at[r], to_xp if up else to_xm, 1)

    def col_here(r):
        arrive(cols.at[r], r_col.at[r])

    def preps(lo, hi):
        def chunk(u, carry):
            @pl.when(u + AHEAD < NS * NZ)
            def _():
                count_copy(u + AHEAD).start()

            count_copy(u).wait()
            q = in_turn(u)

            def part(i, carry):
                at = pl.ds(pl.multiple_of(i * 128, 128), 128)
                n = cnt[pl.ds(pl.multiple_of(q * 4 * B + i * 128, 128), 128), :].astype(F32)
                m = jnp.maximum(n, 1.0)
                conf = jnp.where(n > 0, 0.4 + m * lax.rsqrt(m), 0.0)
                PA[q, at, :] = conf
                PB[q, at, :] = 0.5 * conf * jnp.log(m)
                return carry

            return lax.fori_loop(0, 4 * B // 128, part, carry)

        lax.fori_loop(lo, hi, chunk, 0)

    def halves(s, a, b):
        return jnp.concatenate([a[:, s * B : (s + 1) * B], b[:, s * B : (s + 1) * B]], axis=1)

    def col_lines():
        lines = [line_of(cols[r, 2 * B :]) for r in range(2 * XN)]
        for s in range(NS):
            for j in range(CN // 128):
                LC[s, :, j * 128 : (j + 1) * 128] = halves(s, lines[2 * j], lines[2 * j + 1])

    def lift(p):
        lines = [line_of(rows[p + q, y, k, 2 * B :]) for q in range(2) for y in range(2) for k in range(2)]
        wide = jnp.concatenate(lines, axis=0).T
        for i in range(8):
            for s in range(NS):
                column = wide[s * B : (s + 1) * B, i : i + 1]
                LRB[s, p + i // 4, i % 4 * B : (i % 4 + 1) * B, :] = jnp.broadcast_to(column, (B, 128))

    def turn(s):
        own = cols[:, s * B : (s + 1) * B, :].reshape(CN, D)
        colsC[s] = own
        colsT[s] = (own * 0.5).T
        CPT[s] = jnp.zeros_like(CPT[s])

    def unit(s, p):
        pair = pl.ds(p, 2)
        left = rows[pair, :, :, pl.ds(pl.multiple_of(s * B, B), B), :].reshape(8 * B, D)
        lr = LRB[s, pair].reshape(8 * B, 128)
        t = dot(left, colsT[s], NN) + jnp.concatenate([lr] * (CN // 128), axis=1) + LC[s]
        conf = PA[pl.ds(s * NZ + p, 2)].reshape(8 * B, CN)
        plain = PB[pl.ds(s * NZ + p, 2)].reshape(8 * B, CN)
        g = jnp.where(conf > 0, conf * t - plain, jnp.tanh(t) + 1.0).astype(BF16)
        RP[...] = dot(g, colsC[s], NN).reshape(2, 2, 2, B, D)
        OWN[s, pair] = RP[:, :, c]
        CS[s, pair] = RP[:, :, oc].astype(BF16)
        CPT[s] += dot(left.T, g, NN)

    def sums_here(s, j):
        arrive(CR.at[s, pl.ds(2 * j, 2)], r_cr.at[s, j])

    def chip_sum(s, r):
        return OWN[s, place(r)] + CR[s, place(r)].astype(F32)

    def ring(s, d):
        if d > 0:
            sums_here(s, d - 1)
        if d == H:
            v = chip_sum(s, H)
            RSp[s, H - 1, 0] = v[0].astype(BF16)
            send(RSp.at[s, H - 1, 0], RRp.at[s, H - 1, 0], r_rp.at[s, H - 1], to_zp, 0, 1)
            RSm[s, H - 1, 1] = v[1].astype(BF16)
            send(RSm.at[s, H - 1, 1], RRm.at[s, H - 1, 1], r_rm.at[s, H - 1], to_zm, 0, 1)
        elif d > 0:
            for up in (True, False):
                RS, RR, rr, dev = (RSp, RRp, r_rp, to_zp) if up else (RSm, RRm, r_rm, to_zm)
                v = chip_sum(s, d if up else -d)
                if d == H - 1:
                    half = 0 if up else 1
                    arrive(RR.at[s, d, half], rr.at[s, d])
                    RS[s, d - 1, half] = (v[half] + RR[s, d, half].astype(F32)).astype(BF16)
                    RS[s, d - 1, 1 - half] = v[1 - half].astype(BF16)
                else:
                    arrive(RR.at[s, d], rr.at[s, d])
                    RS[s, d - 1] = (v + RR[s, d].astype(F32)).astype(BF16)
                send(RS.at[s, d - 1], RR.at[s, d - 1], rr.at[s, d - 1], dev, 0, 2)
        else:
            v = chip_sum(s, 0)
            arrive(RRp.at[s, 0], r_rp.at[s, 0])
            arrive(RRm.at[s, 0], r_rm.at[s, 0])
            VR[s] = v + RRp[s, 0].astype(F32) + RRm[s, 0].astype(F32)
            YS[s] = VR[s, 1 - yh].astype(BF16)
            send(YS.at[s], YR.at[s], r_y.at[s], to_yh, 0, 1)

    def out_copy(k, s):
        src, dst = ((gr, nr), (gc, nc))[k]
        return pltpu.make_async_copy(src.at[s], dst.at[s], s_out.at[k, s])

    def rows_out(s):
        arrive(YR.at[s], r_y.at[s])
        gr[s] = 0.5 * (VR[s, yh] + YR[s].astype(F32))
        out_copy(0, s).start()

    def col_far(s):
        CP[s] = CPT[s].T.reshape(2 * XN, B, D)
        Q1s[s, 0] = CP[s, yl * XN + x2].astype(BF16)
        send(Q1s.at[s, 0], Q1r.at[s, 0], r_q.at[s, 0], to_xp, 0, 1)
        Q1s[s, 1] = CP[s, (1 - yl) * XN + x2].astype(BF16)
        send(Q1s.at[s, 1], Q1r.at[s, 1], r_q.at[s, 1], to_xm, 0, 1)

    def col_near(s):
        arrive(Q1r.at[s, 0], r_q.at[s, 0])
        Q2s[s, 0, 0] = (CP[s, yl * XN + xp] + Q1r[s, 0].astype(F32)).astype(BF16)
        Q2s[s, 0, 1] = CP[s, (1 - yl) * XN + xp].astype(BF16)
        send(Q2s.at[s, 0], Q2r.at[s, 0], r_q.at[s, 2], to_xp, 0, 2)
        arrive(Q1r.at[s, 1], r_q.at[s, 1])
        Q2s[s, 1, 0] = CP[s, yl * XN + xm].astype(BF16)
        Q2s[s, 1, 1] = (CP[s, (1 - yl) * XN + xm] + Q1r[s, 1].astype(F32)).astype(BF16)
        send(Q2s.at[s, 1], Q2r.at[s, 1], r_q.at[s, 3], to_xm, 0, 2)

    def col_own(s):
        arrive(Q2r.at[s, 0], r_q.at[s, 2])
        arrive(Q2r.at[s, 1], r_q.at[s, 3])
        Q3s[s] = (CP[s, r_oth] + Q2r[s, 0, 1].astype(F32) + Q2r[s, 1, 1].astype(F32)).astype(BF16)
        send(Q3s.at[s], Q3r.at[s], r_q.at[s, 4], to_yl, 0, 1)
        VC[s] = CP[s, r_own] + Q2r[s, 0, 0].astype(F32) + Q2r[s, 1, 0].astype(F32)

    def cols_out(s):
        arrive(Q3r.at[s], r_q.at[s, 4])
        gc[s] = 0.5 * (VC[s] + Q3r[s].astype(F32))
        out_copy(1, s).start()

    send(row_block(0, 0), row_block(0, 0), r_row.at[0, 1], to_yh, 1)
    send_row(0, 0, True)
    send_row(0, 0, False)
    send(cols.at[r_own], cols.at[r_own], r_col.at[r_own], to_yl, 1)
    send_col(r_own, True)
    send_col(r_own, False)
    preps(0, 3)
    row_step(0, 1)
    col_here(r_oth)
    send_col(r_oth, True)
    send_col(r_oth, False)
    preps(3, 6)
    row_here(1, 0)
    send_row(1, 0, True)
    send_row(1, 0, False)
    preps(6, 8)
    row_step(0, 2)
    col_here(yl * XN + xp)
    send_col(yl * XN + xp, False)
    col_here((1 - yl) * XN + xm)
    send_col((1 - yl) * XN + xm, True)
    preps(8, 11)
    row_step(1, 1)
    row_core(0)
    preps(11, 13)
    row_step(0, 3)
    col_here((1 - yl) * XN + xp)
    col_here(yl * XN + xm)
    col_here(yl * XN + x2)
    col_here((1 - yl) * XN + x2)
    col_lines()
    turn(0)
    turn(1)

    def before(i):
        if i == 1:
            row_step(1, 2)
            row_core(1)
        if i == 2:
            far_out()
            preps(13, 15)
        if i == 3:
            row_step(1, 3)
            row_core(2)
        if i == 4:
            preps(15, 16)
        if i == 5:
            row_here(1, H)
            row_core(3)
        if i % 2 == 0:
            core_here(i // 2)
            lift(i)

    def step(i, carry):
        for k in range(2 * H):
            pl.when(i == k)(functools.partial(before, k))
        s = lax.rem(i, 2)
        j = i // 2
        p = 2 * j
        unit(s, p)
        part = pl.ds(p, 2)
        send(CS.at[s, part], CR.at[s, part], r_cr.at[s, j], to_core, 0)
        return carry

    lax.fori_loop(0, 2 * H, step, 0)
    ring(0, H)
    col_far(0)
    ring(1, H)
    col_far(1)
    ring(0, 3)
    ring(1, 3)
    col_near(0)
    col_near(1)
    ring(0, 2)
    ring(1, 2)
    col_own(0)
    col_own(1)
    ring(0, 1)
    ring(1, 1)
    cols_out(0)
    cols_out(1)
    ring(0, 0)
    ring(1, 0)
    rows_out(0)
    rows_out(1)
    for k in range(2):
        for s in range(NS):
            out_copy(k, s).wait()
    whole = B * D * 2 // (CN * 4)
    gathered = whole * 2 + 16 * D * 2 // (CN * 4)
    arrive(cnt.at[pl.ds(0, total[0] * gathered + (summed[0] + 8 * 2 * H // 2) * whole)], s_all)


def local(counts, re, ce, rm, cm, ra, ca, *, NZ, XN):
    S, B, D = re.shape
    CB = counts.shape[2]
    H = NZ // 2
    R = 2 * XN
    counts = counts.reshape(S, NZ, 4 * B, CB)
    sem = pltpu.SemaphoreType.DMA
    v = pltpu.VMEM
    scratch = [
        v((S, B, D), F32),
        v((S, B, D), F32),
        v((S, B), jnp.int32),
        v((S, B), jnp.int32),
        v((S * NZ * 4 * B, CB), jnp.int32),
        v((NZ, 2, 2, 2 * B + 16, D), BF16),
        v((R, 2 * B + 16, D), BF16),
        v((S, D, CB), BF16),
        v((S, CB, D), BF16),
        v((S, NZ, 4 * B, 128), F32),
        v((S, 1, CB), F32),
        v((S * NZ, 4 * B, CB), F32),
        v((S * NZ, 4 * B, CB), F32),
        v((2, 2, 2, B, D), F32),
        v((S, NZ, 2, B, D), F32),
        v((S, D, CB), F32),
        v((S, R, B, D), F32),
        v((S, NZ, 2, B, D), BF16),
        v((S, NZ, 2, B, D), BF16),
        v((S, H, 2, B, D), BF16),
        v((S, H, 2, B, D), BF16),
        v((S, H, 2, B, D), BF16),
        v((S, H, 2, B, D), BF16),
        v((S, B, D), BF16),
        v((S, B, D), BF16),
        v((S, 2, B, D), F32),
        v((S, 2, B, D), BF16),
        v((S, 2, B, D), BF16),
        v((S, 2, 2, B, D), BF16),
        v((S, 2, 2, B, D), BF16),
        v((S, B, D), BF16),
        v((S, B, D), BF16),
        v((S, B, D), F32),
        v((S, B, D), F32),
        v((S, B, D), F32),
        sem((4,)),
        sem((S * NZ,)),
        sem(()),
        sem((2, S)),
        sem((NZ, 2)),
        sem((H,)),
        sem((R,)),
        sem((S, H)),
        sem((S, H)),
        sem((S, H)),
        sem((S,)),
        sem((S, 5)),
    ]
    gr, gc = pl.pallas_call(
        functools.partial(kernel, NZ, XN, B, D, CB),
        out_shape=(jax.ShapeDtypeStruct((S, B, D), F32), jax.ShapeDtypeStruct((S, B, D), F32)),
        in_specs=[pl.BlockSpec(memory_space=pltpu.HBM)] * 5,
        out_specs=(pl.BlockSpec(memory_space=pltpu.HBM),) * 2,
        scratch_shapes=scratch,
        compiler_params=pltpu.CompilerParams(
            collective_id=0, has_side_effects=True, vmem_limit_bytes=60 * 1024 * 1024
        ),
    )(counts, re, ce, rm, cm)
    return adagrad(re, ra, gr), adagrad(ce, ca, gc)


def solution(mesh):
    return jax.shard_map(
        functools.partial(local, NZ=mesh.shape["col"] // 4, XN=mesh.shape["row"] // 2),
        mesh=mesh,
        in_specs=(
            P(None, "row", "col"),
            P(None, ("row", "col"), None),
            P(None, ("col", "row"), None),
            P(None, ("row", "col")),
            P(None, ("col", "row")),
            P(None, ("row", "col"), None),
            P(None, ("col", "row"), None),
        ),
        out_specs=(P(None, ("row", "col"), None), P(None, ("col", "row"), None)),
        check_vma=False,
    )
```

time: 58.1 us -> 55.4 us (0.954)
  the two profiles are of different devices: /device:TPU:32 before, /device:TPU:8 now
where the time goes in v4:
time: 55.4 us; the launch traced here: 55 us
  Pallas kernels  52.6 us (95%)
  other arithmetic  1.72 us (3%)
  between operations  0.7 us (1%)
    pallas_call x1, Pallas kernels, local(): pl.pallas_call(functools.partial(kernel, NZ, XN, B, D, CB), out_shape=(ja...  52.6 us
    sub x1, other arithmetic, adagrad(): return w - g / jnp.sqrt(a + g * g)  1.72 us

profile of v4, /device:TPU:8, one launch (start us, length us, event | category | flops | bytes accessed | tf_op | source)
XLA Modules:
  0.0 55.0 jit_solution(17918693714398396868)
XLA Ops:
  0.6 0.0 copy-start
  0.6 0.0 copy-start.1
  0.7 0.0 copy-start.2
  0.7 0.0 copy-start.3
  0.7 52.6 %shard_map.86 = (f32[2,64,256]{2,1,0:T(8,128)}, f32[2,64,256]{2,1,0:T(8,128)}) custom-call(s32[2,8,256,512]{3,2,1,0:T(8,128)} %bitcast.1, f32[2,64,256]{2,1,0:T(8,128)} %re_h.1, f32[2,64,256]{2,1,0:T(8,128)} %ce_h.1, s32[2,64]{1,0:T(2,128)} %rm_h.1, s32[2,64]{1,0:T(2,128)} %cm_h.1), custom_call_target="tpu_custom_call" | custom-call | tf_op jit(solution)/shard_map/pallas_call | solution.py:453
  53.3 0.0 copy-done
  53.3 0.0 copy-done.1
  53.3 0.0 copy-done.2
  53.3 0.0 copy-done.3
  53.3 1.7 %multiply_subtract_fusion = (f32[2,64,256]{2,1,0:T(8,128)}, f32[2,64,256]{2,1,0:T(8,128)}) fusion(f32[2,64,256]{2,1,0:T(8,128)S(1)} %copy-done, f32[2,64,256]{2,1,0:T(8,128)} %get-tuple-element.5, f32[2,64,256]{2,1,0:T(8,128)S(1)} %copy-done.2, f32[2,64,256]{2,1,0:T(8,128)S(1)} %copy-done.1, f32[2,64,256]{2,1,0:T(8,128)} %get-tuple-element.4, ...), kind=kLoop, calls=%fused_computation | loop fusion | flops 262144 | bytes 1048576 | tf_op jit(solution)/shard_map/sub | solution.py:23
Async XLA Ops:
  0.6 52.7 %copy-start = (f32[2,64,256]{2,1,0:T(8,128)S(1)}, f32[2,64,256]{2,1,0:T(8,128)}, u32[]{:S(2)}) copy-start(f32[2,64,256]{2,1,0:T(8,128)} %ce_h.1) | copy-start | bytes 393220
  0.6 52.7 %copy-start.1 = (f32[2,64,256]{2,1,0:T(8,128)S(1)}, f32[2,64,256]{2,1,0:T(8,128)}, u32[]{:S(2)}) copy-start(f32[2,64,256]{2,1,0:T(8,128)} %re_h.1) | copy-start | bytes 393220
  0.7 52.7 %copy-start.2 = (f32[2,64,256]{2,1,0:T(8,128)S(1)}, f32[2,64,256]{2,1,0:T(8,128)}, u32[]{:S(2)}) copy-start(f32[2,64,256]{2,1,0:T(8,128)} %param.13) | copy-start | bytes 393220
  0.7 52.7 %copy-start.3 = (f32[2,64,256]{2,1,0:T(8,128)S(1)}, f32[2,64,256]{2,1,0:T(8,128)}, u32[]{:S(2)}) copy-start(f32[2,64,256]{2,1,0:T(8,128)} %param.12) | copy-start | bytes 393220

commit v5 on v4

--- a/solution.py
+++ b/solution.py
@@ -27,7 +27,7 @@
     NZ, XN, B, D, CN,
     counts, re_h, ce_h, rm_h, cm_h, nr, nc,
     re, ce, rm, cm,
-    cnt, rows, cols, colsT, colsC, LRB, LC, PA, PB, RP, OWN, CPT, CP,
+    cnt, rows, cols, colsT, colsC, LRB, LC, PA, PB, RP, CPT, CP,
     CS, CR, RSp, RSm, RRp, RRm, YS, YR, VR, Q1s, Q1r, Q2s, Q2r, Q3s, Q3r, VC, gr, gc,
     s_in, s_cnt, s_all, s_out, r_row, r_core, r_col, r_cr, r_rp, r_rm, r_y, r_q,
 ):
@@ -95,8 +95,13 @@
     for dev in partners:
         pl.semaphore_signal(barrier, inc=1, device_id=dev, device_id_type=MESH)
 
+    def turn_of(i):
+        first, second, late = (i + 7) // 8, (i + 6) // 8, (i + 3) // 8
+        return late + first - second, (1 - late) * (i - first) + late * (8 - i)
+
     def in_turn(u):
-        return lax.rem(u // 2, 2) * NZ + u // 4 * 2 + lax.rem(u, 2)
+        s, j = turn_of(u // 2)
+        return s * NZ + 2 * j + lax.rem(u, 2)
 
     def count_copy(u):
         q = in_turn(u)
@@ -221,16 +226,15 @@
         conf = PA[pl.ds(s * NZ + p, 2)].reshape(8 * B, CN)
         plain = PB[pl.ds(s * NZ + p, 2)].reshape(8 * B, CN)
         g = jnp.where(conf > 0, conf * t - plain, jnp.tanh(t) + 1.0).astype(BF16)
-        RP[...] = dot(g, colsC[s], NN).reshape(2, 2, 2, B, D)
-        OWN[s, pair] = RP[:, :, c]
-        CS[s, pair] = RP[:, :, oc].astype(BF16)
+        RP[s, pair] = dot(g, colsC[s], NN).reshape(2, 2, 2, B, D)
+        CS[s, pair] = RP[s, pair, :, oc].astype(BF16)
         CPT[s] += dot(left.T, g, NN)
 
     def sums_here(s, j):
         arrive(CR.at[s, pl.ds(2 * j, 2)], r_cr.at[s, j])
 
     def chip_sum(s, r):
-        return OWN[s, place(r)] + CR[s, place(r)].astype(F32)
+        return RP[s, place(r), :, c] + CR[s, place(r)].astype(F32)
 
     def ring(s, d):
         if d > 0:
@@ -321,10 +325,10 @@
     send_col(yl * XN + xp, False)
     col_here((1 - yl) * XN + xm)
     send_col((1 - yl) * XN + xm, True)
-    preps(8, 11)
+    preps(8, 9)
     row_step(1, 1)
     row_core(0)
-    preps(11, 13)
+    preps(9, 10)
     row_step(0, 3)
     col_here((1 - yl) * XN + xp)
     col_here(yl * XN + xm)
@@ -335,29 +339,40 @@
     turn(1)
 
     def before(i):
+        if i == 0:
+            core_here(0)
+            lift(0)
         if i == 1:
             row_step(1, 2)
             row_core(1)
         if i == 2:
             far_out()
-            preps(13, 15)
+            core_here(1)
+            lift(2)
         if i == 3:
             row_step(1, 3)
             row_core(2)
+            preps(10, 12)
+            core_here(2)
+            lift(4)
         if i == 4:
-            preps(15, 16)
-        if i == 5:
             row_here(1, H)
             row_core(3)
-        if i % 2 == 0:
-            core_here(i // 2)
-            lift(i)
+            preps(12, 14)
+            core_here(3)
+            lift(6)
+        if i == 6:
+            ring(0, H)
+            col_far(0)
+            preps(14, 16)
+        if i == 7:
+            ring(1, H)
+            ring(0, 3)
 
     def step(i, carry):
         for k in range(2 * H):
             pl.when(i == k)(functools.partial(before, k))
-        s = lax.rem(i, 2)
-        j = i // 2
+        s, j = turn_of(i)
         p = 2 * j
         unit(s, p)
         part = pl.ds(p, 2)
@@ -365,25 +380,21 @@
         return carry
 
     lax.fori_loop(0, 2 * H, step, 0)
-    ring(0, H)
-    col_far(0)
-    ring(1, H)
-    col_far(1)
-    ring(0, 3)
     ring(1, 3)
     col_near(0)
-    col_near(1)
     ring(0, 2)
+    col_far(1)
     ring(1, 2)
     col_own(0)
-    col_own(1)
     ring(0, 1)
+    col_near(1)
     ring(1, 1)
     cols_out(0)
-    cols_out(1)
     ring(0, 0)
+    col_own(1)
     ring(1, 0)
     rows_out(0)
+    cols_out(1)
     rows_out(1)
     for k in range(2):
         for s in range(NS):
@@ -415,8 +426,7 @@
         v((S, 1, CB), F32),
         v((S * NZ, 4 * B, CB), F32),
         v((S * NZ, 4 * B, CB), F32),
-        v((2, 2, 2, B, D), F32),
-        v((S, NZ, 2, B, D), F32),
+        v((S, NZ, 2, 2, B, D), F32),
         v((S, D, CB), F32),
         v((S, R, B, D), F32),
         v((S, NZ, 2, B, D), BF16),

time: 55.4 us -> 55.2 us (level)
  no operation moved by 1% of the time
where the time goes in v5:
time: 55.2 us; the launch traced here: 55 us
  Pallas kernels  52.6 us (95%)
  other arithmetic  1.72 us (3%)
  between operations  0.7 us (1%)
    pallas_call x1, Pallas kernels, local(): pl.pallas_call(functools.partial(kernel, NZ, XN, B, D, CB), out_shape=(ja...  52.6 us
    sub x1, other arithmetic, adagrad(): return w - g / jnp.sqrt(a + g * g)  1.72 us

profile of v5, /device:TPU:8, one launch (start us, length us, event | category | flops | bytes accessed | tf_op | source)
XLA Modules:
  0.0 55.0 jit_solution(6040050918850644813)
XLA Ops:
  0.6 0.0 copy-start
  0.6 0.0 copy-start.1
  0.7 0.0 copy-start.2
  0.7 0.0 copy-start.3
  0.7 52.6 %shard_map.86 = (f32[2,64,256]{2,1,0:T(8,128)}, f32[2,64,256]{2,1,0:T(8,128)}) custom-call(s32[2,8,256,512]{3,2,1,0:T(8,128)} %bitcast.1, f32[2,64,256]{2,1,0:T(8,128)} %re_h.1, f32[2,64,256]{2,1,0:T(8,128)} %ce_h.1, s32[2,64]{1,0:T(2,128)} %rm_h.1, s32[2,64]{1,0:T(2,128)} %cm_h.1), custom_call_target="tpu_custom_call" | custom-call | tf_op jit(solution)/shard_map/pallas_call | solution.py:463
  53.2 0.0 copy-done
  53.3 0.0 copy-done.1
  53.3 0.0 copy-done.2
  53.3 0.0 copy-done.3
  53.3 1.7 %multiply_subtract_fusion = (f32[2,64,256]{2,1,0:T(8,128)}, f32[2,64,256]{2,1,0:T(8,128)}) fusion(f32[2,64,256]{2,1,0:T(8,128)S(1)} %copy-done, f32[2,64,256]{2,1,0:T(8,128)} %get-tuple-element.5, f32[2,64,256]{2,1,0:T(8,128)S(1)} %copy-done.2, f32[2,64,256]{2,1,0:T(8,128)S(1)} %copy-done.1, f32[2,64,256]{2,1,0:T(8,128)} %get-tuple-element.4, ...), kind=kLoop, calls=%fused_computation | loop fusion | flops 262144 | bytes 1048576 | tf_op jit(solution)/shard_map/sub | solution.py:23
Async XLA Ops:
  0.6 52.6 %copy-start = (f32[2,64,256]{2,1,0:T(8,128)S(1)}, f32[2,64,256]{2,1,0:T(8,128)}, u32[]{:S(2)}) copy-start(f32[2,64,256]{2,1,0:T(8,128)} %ce_h.1) | copy-start | bytes 393220
  0.6 52.6 %copy-start.1 = (f32[2,64,256]{2,1,0:T(8,128)S(1)}, f32[2,64,256]{2,1,0:T(8,128)}, u32[]{:S(2)}) copy-start(f32[2,64,256]{2,1,0:T(8,128)} %re_h.1) | copy-start | bytes 393220
  0.7 52.6 %copy-start.2 = (f32[2,64,256]{2,1,0:T(8,128)S(1)}, f32[2,64,256]{2,1,0:T(8,128)}, u32[]{:S(2)}) copy-start(f32[2,64,256]{2,1,0:T(8,128)} %param.13) | copy-start | bytes 393220
  0.7 52.6 %copy-start.3 = (f32[2,64,256]{2,1,0:T(8,128)S(1)}, f32[2,64,256]{2,1,0:T(8,128)}, u32[]{:S(2)}) copy-start(f32[2,64,256]{2,1,0:T(8,128)} %param.12) | copy-start | bytes 393220

commit v6 on v5

--- a/solution.py
+++ b/solution.py
@@ -71,14 +71,12 @@
     rel += [H]
 
     total = [0]
-    summed = [0]
-
-    def send(src, dst, rsem, dev, blocks, sums=0):
+
+    def send(src, dst, rsem, dev, kind, count=1):
         pltpu.make_async_remote_copy(
             src_ref=src, dst_ref=dst, send_sem=s_all, recv_sem=rsem, device_id=dev, device_id_type=MESH
         ).start()
-        total[0] += blocks
-        summed[0] += sums
+        total[0] += count * (B + 16 if kind == 0 else B)
 
     def arrive(dst, rsem):
         pltpu.make_async_copy(dst, dst, rsem).wait()
@@ -131,8 +129,8 @@
 
     for ref, parts in ((rows.at[0, yh, c], own_block(re, rm, 20.0)), (cols.at[r_own], own_block(ce, cm, 0.0))):
         ref[0:B] = parts[0]
-        ref[B : 2 * B] = parts[1]
-        ref[2 * B :] = parts[2]
+        ref[B : B + 16] = parts[2]
+        ref[B + 16 :] = parts[1]
 
     def line_of(tail):
         tail = tail.astype(F32)
@@ -140,38 +138,66 @@
 
     pl.semaphore_wait(barrier, len(partners))
 
-    def row_block(p, y):
-        return rows.at[p, 1 - yh if y else yh, c]
-
-    def send_row(y, r, up):
+    def part(s):
+        return pl.ds(0, B + 16) if s == 0 else pl.ds(B + 16, B)
+
+    def row_block(s, p, y):
+        return rows.at[p, 1 - yh if y else yh, c, part(s)]
+
+    def send_row(s, y, r, up):
         to = place_of(r - 1 if up else r + 1)
-        send(row_block(place(r), y), row_block(to, y), r_row.at[to, y], to_zp if up else to_zm, 1)
-
-    def row_here(y, r):
-        arrive(row_block(place_of(r), y), r_row.at[place_of(r), y])
-
-    def row_step(y, d):
+        send(row_block(s, place(r), y), row_block(s, to, y), r_row.at[s, to, y], to_zp if up else to_zm, s)
+
+    def row_here(s, y, r):
+        arrive(row_block(s, place_of(r), y), r_row.at[s, place_of(r), y])
+
+    def row_step(s, y, d):
         for sign in (-1, 1):
-            row_here(y, sign * d)
+            row_here(s, y, sign * d)
             if d < H - 1 or (y == 0 and sign < 0):
-                send_row(y, sign * d, sign < 0)
-
-    def far_out():
-        row_here(0, H)
-        send(row_block(NZ - 1, 0), row_block(NZ - 1, 0), r_row.at[NZ - 1, 1], to_yh, 1)
-
-    def row_core(j):
-        ref = rows.at[pl.ds(2 * j, 2), :, c]
-        send(ref, ref, r_core.at[j], to_core, 4)
-
-    def core_here(j):
-        arrive(rows.at[pl.ds(2 * j, 2), :, oc], r_core.at[j])
-
-    def send_col(r, up):
-        send(cols.at[r], cols.at[r], r_col.at[r], to_xp if up else to_xm, 1)
-
-    def col_here(r):
-        arrive(cols.at[r], r_col.at[r])
+                send_row(s, y, sign * d, sign < 0)
+
+    def row_y(s):
+        row_here(s, 1, 0)
+        send_row(s, 1, 0, True)
+        send_row(s, 1, 0, False)
+
+    def far_out(s):
+        row_here(s, 0, H)
+        send(row_block(s, NZ - 1, 0), row_block(s, NZ - 1, 0), r_row.at[s, NZ - 1, 1], to_yh, s)
+
+    def row_core(s, j):
+        ref = rows.at[pl.ds(2 * j, 2), :, c, part(s)]
+        send(ref, ref, r_core.at[s, j], to_core, s, 4)
+
+    def core_here(s, j):
+        arrive(rows.at[pl.ds(2 * j, 2), :, oc, part(s)], r_core.at[s, j])
+
+    def col_block(s, r):
+        return cols.at[r, part(s)]
+
+    def send_col(s, r, up):
+        send(col_block(s, r), col_block(s, r), r_col.at[s, r], to_xp if up else to_xm, s)
+
+    def col_here(s, r):
+        arrive(col_block(s, r), r_col.at[s, r])
+
+    def col_y(s):
+        col_here(s, r_oth)
+        send_col(s, r_oth, True)
+        send_col(s, r_oth, False)
+
+    def col_x(s):
+        col_here(s, yl * XN + xp)
+        send_col(s, yl * XN + xp, False)
+        col_here(s, (1 - yl) * XN + xm)
+        send_col(s, (1 - yl) * XN + xm, True)
+
+    def all_cols(s):
+        col_here(s, (1 - yl) * XN + xp)
+        col_here(s, yl * XN + xm)
+        col_here(s, yl * XN + x2)
+        col_here(s, (1 - yl) * XN + x2)
 
     def preps(lo, hi):
         def chunk(u, carry):
@@ -199,13 +225,13 @@
         return jnp.concatenate([a[:, s * B : (s + 1) * B], b[:, s * B : (s + 1) * B]], axis=1)
 
     def col_lines():
-        lines = [line_of(cols[r, 2 * B :]) for r in range(2 * XN)]
+        lines = [line_of(cols[r, B : B + 16]) for r in range(2 * XN)]
         for s in range(NS):
             for j in range(CN // 128):
                 LC[s, :, j * 128 : (j + 1) * 128] = halves(s, lines[2 * j], lines[2 * j + 1])
 
     def lift(p):
-        lines = [line_of(rows[p + q, y, k, 2 * B :]) for q in range(2) for y in range(2) for k in range(2)]
+        lines = [line_of(rows[p + q, y, k, B : B + 16]) for q in range(2) for y in range(2) for k in range(2)]
         wide = jnp.concatenate(lines, axis=0).T
         for i in range(8):
             for s in range(NS):
@@ -213,14 +239,14 @@
                 LRB[s, p + i // 4, i % 4 * B : (i % 4 + 1) * B, :] = jnp.broadcast_to(column, (B, 128))
 
     def turn(s):
-        own = cols[:, s * B : (s + 1) * B, :].reshape(CN, D)
+        own = cols[:, s * (B + 16) : s * (B + 16) + B, :].reshape(CN, D)
         colsC[s] = own
         colsT[s] = (own * 0.5).T
         CPT[s] = jnp.zeros_like(CPT[s])
 
     def unit(s, p):
         pair = pl.ds(p, 2)
-        left = rows[pair, :, :, pl.ds(pl.multiple_of(s * B, B), B), :].reshape(8 * B, D)
+        left = rows[pair, :, :, pl.ds(pl.multiple_of(s * (B + 16), 16), B), :].reshape(8 * B, D)
         lr = LRB[s, pair].reshape(8 * B, 128)
         t = dot(left, colsT[s], NN) + jnp.concatenate([lr] * (CN // 128), axis=1) + LC[s]
         conf = PA[pl.ds(s * NZ + p, 2)].reshape(8 * B, CN)
@@ -242,9 +268,9 @@
         if d == H:
             v = chip_sum(s, H)
             RSp[s, H - 1, 0] = v[0].astype(BF16)
-            send(RSp.at[s, H - 1, 0], RRp.at[s, H - 1, 0], r_rp.at[s, H - 1], to_zp, 0, 1)
+            send(RSp.at[s, H - 1, 0], RRp.at[s, H - 1, 0], r_rp.at[s, H - 1], to_zp, 1, 1)
             RSm[s, H - 1, 1] = v[1].astype(BF16)
-            send(RSm.at[s, H - 1, 1], RRm.at[s, H - 1, 1], r_rm.at[s, H - 1], to_zm, 0, 1)
+            send(RSm.at[s, H - 1, 1], RRm.at[s, H - 1, 1], r_rm.at[s, H - 1], to_zm, 1, 1)
         elif d > 0:
             for up in (True, False):
                 RS, RR, rr, dev = (RSp, RRp, r_rp, to_zp) if up else (RSm, RRm, r_rm, to_zm)
@@ -257,14 +283,14 @@
                 else:
                     arrive(RR.at[s, d], rr.at[s, d])
                     RS[s, d - 1] = (v + RR[s, d].astype(F32)).astype(BF16)
-                send(RS.at[s, d - 1], RR.at[s, d - 1], rr.at[s, d - 1], dev, 0, 2)
+                send(RS.at[s, d - 1], RR.at[s, d - 1], rr.at[s, d - 1], dev, 1, 2)
         else:
             v = chip_sum(s, 0)
             arrive(RRp.at[s, 0], r_rp.at[s, 0])
             arrive(RRm.at[s, 0], r_rm.at[s, 0])
             VR[s] = v + RRp[s, 0].astype(F32) + RRm[s, 0].astype(F32)
             YS[s] = VR[s, 1 - yh].astype(BF16)
-            send(YS.at[s], YR.at[s], r_y.at[s], to_yh, 0, 1)
+            send(YS.at[s], YR.at[s], r_y.at[s], to_yh, 1, 1)
 
     def out_copy(k, s):
         src, dst = ((gr, nr), (gc, nc))[k]
@@ -278,25 +304,25 @@
     def col_far(s):
         CP[s] = CPT[s].T.reshape(2 * XN, B, D)
         Q1s[s, 0] = CP[s, yl * XN + x2].astype(BF16)
-        send(Q1s.at[s, 0], Q1r.at[s, 0], r_q.at[s, 0], to_xp, 0, 1)
+        send(Q1s.at[s, 0], Q1r.at[s, 0], r_q.at[s, 0], to_xp, 1, 1)
         Q1s[s, 1] = CP[s, (1 - yl) * XN + x2].astype(BF16)
-        send(Q1s.at[s, 1], Q1r.at[s, 1], r_q.at[s, 1], to_xm, 0, 1)
+        send(Q1s.at[s, 1], Q1r.at[s, 1], r_q.at[s, 1], to_xm, 1, 1)
 
     def col_near(s):
         arrive(Q1r.at[s, 0], r_q.at[s, 0])
         Q2s[s, 0, 0] = (CP[s, yl * XN + xp] + Q1r[s, 0].astype(F32)).astype(BF16)
         Q2s[s, 0, 1] = CP[s, (1 - yl) * XN + xp].astype(BF16)
-        send(Q2s.at[s, 0], Q2r.at[s, 0], r_q.at[s, 2], to_xp, 0, 2)
+        send(Q2s.at[s, 0], Q2r.at[s, 0], r_q.at[s, 2], to_xp, 1, 2)
         arrive(Q1r.at[s, 1], r_q.at[s, 1])
         Q2s[s, 1, 0] = CP[s, yl * XN + xm].astype(BF16)
         Q2s[s, 1, 1] = (CP[s, (1 - yl) * XN + xm] + Q1r[s, 1].astype(F32)).astype(BF16)
-        send(Q2s.at[s, 1], Q2r.at[s, 1], r_q.at[s, 3], to_xm, 0, 2)
+        send(Q2s.at[s, 1], Q2r.at[s, 1], r_q.at[s, 3], to_xm, 1, 2)
 
     def col_own(s):
         arrive(Q2r.at[s, 0], r_q.at[s, 2])
         arrive(Q2r.at[s, 1], r_q.at[s, 3])
         Q3s[s] = (CP[s, r_oth] + Q2r[s, 0, 1].astype(F32) + Q2r[s, 1, 1].astype(F32)).astype(BF16)
-        send(Q3s.at[s], Q3r.at[s], r_q.at[s, 4], to_yl, 0, 1)
+        send(Q3s.at[s], Q3r.at[s], r_q.at[s, 4], to_yl, 1, 1)
         VC[s] = CP[s, r_own] + Q2r[s, 0, 0].astype(F32) + Q2r[s, 1, 0].astype(F32)
 
     def cols_out(s):
@@ -304,70 +330,85 @@
         gc[s] = 0.5 * (VC[s] + Q3r[s].astype(F32))
         out_copy(1, s).start()
 
-    send(row_block(0, 0), row_block(0, 0), r_row.at[0, 1], to_yh, 1)
-    send_row(0, 0, True)
-    send_row(0, 0, False)
-    send(cols.at[r_own], cols.at[r_own], r_col.at[r_own], to_yl, 1)
-    send_col(r_own, True)
-    send_col(r_own, False)
-    preps(0, 3)
-    row_step(0, 1)
-    col_here(r_oth)
-    send_col(r_oth, True)
-    send_col(r_oth, False)
-    preps(3, 6)
-    row_here(1, 0)
-    send_row(1, 0, True)
-    send_row(1, 0, False)
-    preps(6, 8)
-    row_step(0, 2)
-    col_here(yl * XN + xp)
-    send_col(yl * XN + xp, False)
-    col_here((1 - yl) * XN + xm)
-    send_col((1 - yl) * XN + xm, True)
-    preps(8, 9)
-    row_step(1, 1)
-    row_core(0)
-    preps(9, 10)
-    row_step(0, 3)
-    col_here((1 - yl) * XN + xp)
-    col_here(yl * XN + xm)
-    col_here(yl * XN + x2)
-    col_here((1 - yl) * XN + x2)
+    for s in range(NS):
+        send(row_block(s, 0, 0), row_block(s, 0, 0), r_row.at[s, 0, 1], to_yh, s)
+        send_row(s, 0, 0, True)
+        send_row(s, 0, 0, False)
+        send(col_block(s, r_own), col_block(s, r_own), r_col.at[s, r_own], to_yl, s)
+        send_col(s, r_own, True)
+        send_col(s, r_own, False)
+    preps(0, 1)
+    row_step(0, 0, 1)
+    col_y(0)
+    row_y(0)
+    row_step(1, 0, 1)
+    preps(1, 2)
+    row_step(0, 0, 2)
+    col_x(0)
+    row_y(1)
+    col_y(1)
+    row_step(1, 0, 2)
+    preps(2, 3)
+    row_step(0, 1, 1)
+    row_core(0, 0)
+    col_x(1)
+    row_step(0, 0, 3)
+    preps(3, 4)
+    row_step(1, 1, 1)
+    row_core(1, 0)
+    row_step(1, 0, 3)
+    preps(4, 5)
+    all_cols(0)
     col_lines()
     turn(0)
-    turn(1)
+    row_step(0, 1, 2)
+    row_core(0, 1)
+    preps(5, 6)
 
     def before(i):
         if i == 0:
-            core_here(0)
+            core_here(0, 0)
             lift(0)
         if i == 1:
-            row_step(1, 2)
-            row_core(1)
+            far_out(0)
+            row_step(1, 1, 2)
+            row_core(1, 1)
+            all_cols(1)
+            turn(1)
+            core_here(1, 0)
         if i == 2:
-            far_out()
-            core_here(1)
+            row_step(0, 1, 3)
+            row_core(0, 2)
+            far_out(1)
+            core_here(0, 1)
             lift(2)
         if i == 3:
-            row_step(1, 3)
-            row_core(2)
-            preps(10, 12)
-            core_here(2)
+            row_step(1, 1, 3)
+            row_core(1, 2)
+            row_here(0, 1, H)
+            row_core(0, 3)
+            preps(6, 8)
+            core_here(0, 2)
             lift(4)
         if i == 4:
-            row_here(1, H)
-            row_core(3)
-            preps(12, 14)
-            core_here(3)
+            row_here(1, 1, H)
+            row_core(1, 3)
+            preps(8, 10)
+            core_here(0, 3)
             lift(6)
+        if i == 5:
+            preps(10, 12)
+            core_here(1, 3)
         if i == 6:
             ring(0, H)
+            preps(12, 14)
+            core_here(1, 2)
+        if i == 7:
+            ring(1, H)
             col_far(0)
             preps(14, 16)
-        if i == 7:
-            ring(1, H)
             ring(0, 3)
+            core_here(1, 1)
 
     def step(i, carry):
         for k in range(2 * H):
@@ -376,7 +417,7 @@
         p = 2 * j
         unit(s, p)
         part = pl.ds(p, 2)
-        send(CS.at[s, part], CR.at[s, part], r_cr.at[s, j], to_core, 0)
+        send(CS.at[s, part], CR.at[s, part], r_cr.at[s, j], to_core, 1, 4 * 2 * H)
         return carry
 
     lax.fori_loop(0, 2 * H, step, 0)
@@ -399,9 +440,7 @@
     for k in range(2):
         for s in range(NS):
             out_copy(k, s).wait()
-    whole = B * D * 2 // (CN * 4)
-    gathered = whole * 2 + 16 * D * 2 // (CN * 4)
-    arrive(cnt.at[pl.ds(0, total[0] * gathered + (summed[0] + 8 * 2 * H // 2) * whole)], s_all)
+    arrive(cnt.at[pl.ds(0, total[0] * D * 2 // (CN * 4))], s_all)
 
 
 def local(counts, re, ce, rm, cm, ra, ca, *, NZ, XN):
@@ -451,9 +490,9 @@
         sem((S * NZ,)),
         sem(()),
         sem((2, S)),
-        sem((NZ, 2)),
-        sem((H,)),
-        sem((R,)),
+        sem((S, NZ, 2)),
+        sem((S, H)),
+        sem((S, R)),
         sem((S, H)),
         sem((S, H)),
         sem((S, H)),

time: 55.2 us -> 55.8 us (1.011); the launches traced: 55 us -> 54.9 us
  no operation moved by 1% of the time
where the time goes in v6:
time: 55.8 us; the launch traced here: 54.9 us
  Pallas kernels  52.5 us (94%)
  other arithmetic  1.72 us (3%)
  between operations  0.7 us (1%)
    pallas_call x1, Pallas kernels, local(): pl.pallas_call(functools.partial(kernel, NZ, XN, B, D, CB), out_shape=(ja...  52.5 us
    sub x1, other arithmetic, adagrad(): return w - g / jnp.sqrt(a + g * g)  1.72 us

profile of v6, /device:TPU:8, one launch (start us, length us, event | category | flops | bytes accessed | tf_op | source)
XLA Modules:
  0.0 54.9 jit_solution(4258326209145478231)
XLA Ops:
  0.6 0.0 copy-start
  0.6 0.0 copy-start.1
  0.7 0.0 copy-start.2
  0.7 0.0 copy-start.3
  0.7 52.5 %shard_map.86 = (f32[2,64,256]{2,1,0:T(8,128)}, f32[2,64,256]{2,1,0:T(8,128)}) custom-call(s32[2,8,256,512]{3,2,1,0:T(8,128)} %bitcast.1, f32[2,64,256]{2,1,0:T(8,128)} %re_h.1, f32[2,64,256]{2,1,0:T(8,128)} %ce_h.1, s32[2,64]{1,0:T(2,128)} %rm_h.1, s32[2,64]{1,0:T(2,128)} %cm_h.1), custom_call_target="tpu_custom_call" | custom-call | tf_op jit(solution)/shard_map/pallas_call | solution.py:502
  53.1 0.0 copy-done
  53.1 0.0 copy-done.1
  53.2 0.0 copy-done.2
  53.2 0.0 copy-done.3
  53.2 1.7 %multiply_subtract_fusion = (f32[2,64,256]{2,1,0:T(8,128)}, f32[2,64,256]{2,1,0:T(8,128)}) fusion(f32[2,64,256]{2,1,0:T(8,128)S(1)} %copy-done, f32[2,64,256]{2,1,0:T(8,128)} %get-tuple-element.5, f32[2,64,256]{2,1,0:T(8,128)S(1)} %copy-done.2, f32[2,64,256]{2,1,0:T(8,128)S(1)} %copy-done.1, f32[2,64,256]{2,1,0:T(8,128)} %get-tuple-element.4, ...), kind=kLoop, calls=%fused_computation | loop fusion | flops 262144 | bytes 1048576 | tf_op jit(solution)/shard_map/sub | solution.py:23
Async XLA Ops:
  0.6 52.5 %copy-start = (f32[2,64,256]{2,1,0:T(8,128)S(1)}, f32[2,64,256]{2,1,0:T(8,128)}, u32[]{:S(2)}) copy-start(f32[2,64,256]{2,1,0:T(8,128)} %ce_h.1) | copy-start | bytes 393220
  0.6 52.5 %copy-start.1 = (f32[2,64,256]{2,1,0:T(8,128)S(1)}, f32[2,64,256]{2,1,0:T(8,128)}, u32[]{:S(2)}) copy-start(f32[2,64,256]{2,1,0:T(8,128)} %re_h.1) | copy-start | bytes 393220
  0.7 52.5 %copy-start.2 = (f32[2,64,256]{2,1,0:T(8,128)S(1)}, f32[2,64,256]{2,1,0:T(8,128)}, u32[]{:S(2)}) copy-start(f32[2,64,256]{2,1,0:T(8,128)} %param.13) | copy-start | bytes 393220
  0.7 52.5 %copy-start.3 = (f32[2,64,256]{2,1,0:T(8,128)S(1)}, f32[2,64,256]{2,1,0:T(8,128)}, u32[]{:S(2)}) copy-start(f32[2,64,256]{2,1,0:T(8,128)} %param.12) | copy-start | bytes 393220

commit v7 on v6

--- a/solution.py
+++ b/solution.py
@@ -19,14 +19,14 @@
     return lax.dot_general(a, b, dims, preferred_element_type=F32)
 
 
-def adagrad(w, a, g):
-    return w - g / jnp.sqrt(a + g * g)
+def update(g, a):
+    return g / jnp.sqrt(a + g * g)
 
 
 def kernel(
     NZ, XN, B, D, CN,
-    counts, re_h, ce_h, rm_h, cm_h, nr, nc,
-    re, ce, rm, cm,
+    counts, re_h, ce_h, rm_h, cm_h, ra_h, ca_h, nr, nc,
+    re, ce, rm, cm, ra, ca,
     cnt, rows, cols, colsT, colsC, LRB, LC, PA, PB, RP, CPT, CP,
     CS, CR, RSp, RSm, RRp, RRm, YS, YR, VR, Q1s, Q1r, Q2s, Q2r, Q3s, Q3r, VC, gr, gc,
     s_in, s_cnt, s_all, s_out, r_row, r_core, r_col, r_cr, r_rp, r_rm, r_y, r_q,
@@ -83,7 +83,7 @@
 
     own_in = [
         pltpu.make_async_copy(src, dst, s_in.at[i])
-        for i, (src, dst) in enumerate(((rm_h, rm), (cm_h, cm), (re_h, re), (ce_h, ce)))
+        for i, (src, dst) in enumerate(((rm_h, rm), (cm_h, cm), (re_h, re), (ce_h, ce), (ra_h, ra), (ca_h, ca)))
     ]
     for copy in own_in:
         copy.start()
@@ -113,7 +113,7 @@
     for u in range(AHEAD):
         count_copy(u).start()
 
-    for copy in own_in:
+    for copy in own_in[:4]:
         copy.wait()
 
     def own_block(embed, margs, shift):
@@ -127,7 +127,7 @@
         tail = jnp.where(which == 0, upper, jnp.where(which == 1, lower, 0.0)).astype(BF16)
         return embed[0].astype(BF16), embed[1].astype(BF16), tail
 
-    for ref, parts in ((rows.at[0, yh, c], own_block(re, rm, 20.0)), (cols.at[r_own], own_block(ce, cm, 0.0))):
+    for ref, parts in ((rows.at[0, yh, c], own_block(re, rm, 20.0)), (cols.at[yl, x], own_block(ce, cm, 0.0))):
         ref[0:B] = parts[0]
         ref[B : B + 16] = parts[2]
         ref[B + 16 :] = parts[1]
@@ -173,31 +173,26 @@
     def core_here(s, j):
         arrive(rows.at[pl.ds(2 * j, 2), :, oc, part(s)], r_core.at[s, j])
 
-    def col_block(s, r):
-        return cols.at[r, part(s)]
-
-    def send_col(s, r, up):
-        send(col_block(s, r), col_block(s, r), r_col.at[s, r], to_xp if up else to_xm, s)
-
-    def col_here(s, r):
-        arrive(col_block(s, r), r_col.at[s, r])
+    def col_block(s, y, at):
+        return cols.at[y, at, part(s)]
+
+    def col_pair(s, at):
+        return cols.at[:, at, part(s)]
 
     def col_y(s):
-        col_here(s, r_oth)
-        send_col(s, r_oth, True)
-        send_col(s, r_oth, False)
+        arrive(col_block(s, 1 - yl, x), r_col.at[s, 0])
+        send(col_pair(s, x), col_pair(s, x), r_col.at[s, 1], to_xp, s, 2)
+        send(col_pair(s, x), col_pair(s, x), r_col.at[s, 2], to_xm, s, 2)
 
     def col_x(s):
-        col_here(s, yl * XN + xp)
-        send_col(s, yl * XN + xp, False)
-        col_here(s, (1 - yl) * XN + xm)
-        send_col(s, (1 - yl) * XN + xm, True)
+        arrive(col_pair(s, xp), r_col.at[s, 2])
+        send(col_block(s, yl, xp), col_block(s, yl, xp), r_col.at[s, 3], to_xm, s)
+        arrive(col_pair(s, xm), r_col.at[s, 1])
+        send(col_block(s, 1 - yl, xm), col_block(s, 1 - yl, xm), r_col.at[s, 4], to_xp, s)
 
     def all_cols(s):
-        col_here(s, (1 - yl) * XN + xp)
-        col_here(s, yl * XN + xm)
-        col_here(s, yl * XN + x2)
-        col_here(s, (1 - yl) * XN + x2)
+        arrive(col_block(s, yl, x2), r_col.at[s, 3])
+        arrive(col_block(s, 1 - yl, x2), r_col.at[s, 4])
 
     def preps(lo, hi):
         def chunk(u, carry):
@@ -225,7 +220,7 @@
         return jnp.concatenate([a[:, s * B : (s + 1) * B], b[:, s * B : (s + 1) * B]], axis=1)
 
     def col_lines():
-        lines = [line_of(cols[r, B : B + 16]) for r in range(2 * XN)]
+        lines = [line_of(cols[r // XN, r % XN, B : B + 16]) for r in range(2 * XN)]
         for s in range(NS):
             for j in range(CN // 128):
                 LC[s, :, j * 128 : (j + 1) * 128] = halves(s, lines[2 * j], lines[2 * j + 1])
@@ -239,7 +234,7 @@
                 LRB[s, p + i // 4, i % 4 * B : (i % 4 + 1) * B, :] = jnp.broadcast_to(column, (B, 128))
 
     def turn(s):
-        own = cols[:, s * (B + 16) : s * (B + 16) + B, :].reshape(CN, D)
+        own = cols[:, :, s * (B + 16) : s * (B + 16) + B, :].reshape(CN, D)
         colsC[s] = own
         colsT[s] = (own * 0.5).T
         CPT[s] = jnp.zeros_like(CPT[s])
@@ -262,35 +257,55 @@
     def chip_sum(s, r):
         return RP[s, place(r), :, c] + CR[s, place(r)].astype(F32)
 
+    def half_sum(s, r, y):
+        return RP[s, place(r), y, c] + CR[s, place(r), y].astype(F32)
+
+    halves_in_turn = (1 - yh, yh)
+
     def ring(s, d):
         if d > 0:
             sums_here(s, d - 1)
+        lanes_of = ((RSp, RRp, r_rp, to_zp, 1), (RSm, RRm, r_rm, to_zm, -1))
         if d == H:
             v = chip_sum(s, H)
-            RSp[s, H - 1, 0] = v[0].astype(BF16)
-            send(RSp.at[s, H - 1, 0], RRp.at[s, H - 1, 0], r_rp.at[s, H - 1], to_zp, 1, 1)
-            RSm[s, H - 1, 1] = v[1].astype(BF16)
-            send(RSm.at[s, H - 1, 1], RRm.at[s, H - 1, 1], r_rm.at[s, H - 1], to_zm, 1, 1)
+            for half, (RS, RR, rr, dev, _) in enumerate(lanes_of):
+                RS[s, H - 1, half] = v[half].astype(BF16)
+                send(RS.at[s, H - 1, half], RR.at[s, H - 1, half], rr.at[s, H - 1, 0], dev, 1, 1)
+        elif d == H - 1:
+            for half, (RS, RR, rr, dev, sign) in enumerate(lanes_of):
+                v = chip_sum(s, sign * d)
+                arrive(RR.at[s, d, half], rr.at[s, d, 0])
+                RS[s, d - 1, half] = (v[half] + RR[s, d, half].astype(F32)).astype(BF16)
+                RS[s, d - 1, 1 - half] = v[1 - half].astype(BF16)
+                send(RS.at[s, d - 1], RR.at[s, d - 1], rr.at[s, d - 1, 0], dev, 1, 2)
+        elif d > 0 and s == 0:
+            for RS, RR, rr, dev, sign in lanes_of:
+                v = chip_sum(s, sign * d)
+                arrive(RR.at[s, d], rr.at[s, d, 0])
+                RS[s, d - 1] = (v + RR[s, d].astype(F32)).astype(BF16)
+                send(RS.at[s, d - 1], RR.at[s, d - 1], rr.at[s, d - 1, 0], dev, 1, 2)
         elif d > 0:
-            for up in (True, False):
-                RS, RR, rr, dev = (RSp, RRp, r_rp, to_zp) if up else (RSm, RRm, r_rm, to_zm)
-                v = chip_sum(s, d if up else -d)
-                if d == H - 1:
-                    half = 0 if up else 1
-                    arrive(RR.at[s, d, half], rr.at[s, d])
-                    RS[s, d - 1, half] = (v[half] + RR[s, d, half].astype(F32)).astype(BF16)
-                    RS[s, d - 1, 1 - half] = v[1 - half].astype(BF16)
+            for k, y in enumerate(halves_in_turn):
+                for RS, RR, rr, dev, sign in lanes_of:
+                    if d < H - 2:
+                        arrive(RR.at[s, d, y], rr.at[s, d, k])
+                    elif k == 0:
+                        arrive(RR.at[s, d], rr.at[s, d, 0])
+                    RS[s, d - 1, y] = (half_sum(s, sign * d, y) + RR[s, d, y].astype(F32)).astype(BF16)
+                    send(RS.at[s, d - 1, y], RR.at[s, d - 1, y], rr.at[s, d - 1, k], dev, 1, 1)
+        else:
+            for k, y in enumerate(halves_in_turn):
+                for _, RR, rr, _, _ in lanes_of:
+                    if s == 1:
+                        arrive(RR.at[s, 0, y], rr.at[s, 0, k])
+                    elif k == 0:
+                        arrive(RR.at[s, 0], rr.at[s, 0, 0])
+                v = half_sum(s, 0, y) + RRp[s, 0, y].astype(F32) + RRm[s, 0, y].astype(F32)
+                if k == 0:
+                    YS[s] = v.astype(BF16)
+                    send(YS.at[s], YR.at[s], r_y.at[s], to_yh, 1, 1)
                 else:
-                    arrive(RR.at[s, d], rr.at[s, d])
-                    RS[s, d - 1] = (v + RR[s, d].astype(F32)).astype(BF16)
-                send(RS.at[s, d - 1], RR.at[s, d - 1], rr.at[s, d - 1], dev, 1, 2)
-        else:
-            v = chip_sum(s, 0)
-            arrive(RRp.at[s, 0], r_rp.at[s, 0])
-            arrive(RRm.at[s, 0], r_rm.at[s, 0])
-            VR[s] = v + RRp[s, 0].astype(F32) + RRm[s, 0].astype(F32)
-            YS[s] = VR[s, 1 - yh].astype(BF16)
-            send(YS.at[s], YR.at[s], r_y.at[s], to_yh, 1, 1)
+                    VR[s] = v
 
     def out_copy(k, s):
         src, dst = ((gr, nr), (gc, nc))[k]
@@ -298,7 +313,7 @@
 
     def rows_out(s):
         arrive(YR.at[s], r_y.at[s])
-        gr[s] = 0.5 * (VR[s, yh] + YR[s].astype(F32))
+        gr[s] = update(0.5 * (VR[s] + YR[s].astype(F32)), ra[s])
         out_copy(0, s).start()
 
     def col_far(s):
@@ -327,26 +342,24 @@
 
     def cols_out(s):
         arrive(Q3r.at[s], r_q.at[s, 4])
-        gc[s] = 0.5 * (VC[s] + Q3r[s].astype(F32))
+        gc[s] = update(0.5 * (VC[s] + Q3r[s].astype(F32)), ca[s])
         out_copy(1, s).start()
 
     for s in range(NS):
+        send(col_block(s, yl, x), col_block(s, yl, x), r_col.at[s, 0], to_yl, s)
         send(row_block(s, 0, 0), row_block(s, 0, 0), r_row.at[s, 0, 1], to_yh, s)
         send_row(s, 0, 0, True)
         send_row(s, 0, 0, False)
-        send(col_block(s, r_own), col_block(s, r_own), r_col.at[s, r_own], to_yl, s)
-        send_col(s, r_own, True)
-        send_col(s, r_own, False)
     preps(0, 1)
+    col_y(0)
     row_step(0, 0, 1)
-    col_y(0)
     row_y(0)
     row_step(1, 0, 1)
+    col_y(1)
     preps(1, 2)
     row_step(0, 0, 2)
     col_x(0)
     row_y(1)
-    col_y(1)
     row_step(1, 0, 2)
     preps(2, 3)
     row_step(0, 1, 1)
@@ -421,6 +434,8 @@
         return carry
 
     lax.fori_loop(0, 2 * H, step, 0)
+    for copy in own_in[4:]:
+        copy.wait()
     ring(1, 3)
     col_near(0)
     ring(0, 2)
@@ -456,9 +471,11 @@
         v((S, B, D), F32),
         v((S, B), jnp.int32),
         v((S, B), jnp.int32),
+        v((S, B, D), F32),
+        v((S, B, D), F32),
         v((S * NZ * 4 * B, CB), jnp.int32),
         v((NZ, 2, 2, 2 * B + 16, D), BF16),
-        v((R, 2 * B + 16, D), BF16),
+        v((2, XN, 2 * B + 16, D), BF16),
         v((S, D, CB), BF16),
         v((S, CB, D), BF16),
         v((S, NZ, 4 * B, 128), F32),
@@ -476,7 +493,7 @@
         v((S, H, 2, B, D), BF16),
         v((S, B, D), BF16),
         v((S, B, D), BF16),
-        v((S, 2, B, D), F32),
+        v((S, B, D), F32),
         v((S, 2, B, D), BF16),
         v((S, 2, B, D), BF16),
         v((S, 2, 2, B, D), BF16),
@@ -486,30 +503,30 @@
         v((S, B, D), F32),
         v((S, B, D), F32),
         v((S, B, D), F32),
-        sem((4,)),
+        sem((6,)),
         sem((S * NZ,)),
         sem(()),
         sem((2, S)),
         sem((S, NZ, 2)),
         sem((S, H)),
-        sem((S, R)),
+        sem((S, 5)),
         sem((S, H)),
-        sem((S, H)),
-        sem((S, H)),
+        sem((S, H, 2)),
+        sem((S, H, 2)),
         sem((S,)),
         sem((S, 5)),
     ]
     gr, gc = pl.pallas_call(
         functools.partial(kernel, NZ, XN, B, D, CB),
         out_shape=(jax.ShapeDtypeStruct((S, B, D), F32), jax.ShapeDtypeStruct((S, B, D), F32)),
-        in_specs=[pl.BlockSpec(memory_space=pltpu.HBM)] * 5,
+        in_specs=[pl.BlockSpec(memory_space=pltpu.HBM)] * 7,
         out_specs=(pl.BlockSpec(memory_space=pltpu.HBM),) * 2,
         scratch_shapes=scratch,
         compiler_params=pltpu.CompilerParams(
             collective_id=0, has_side_effects=True, vmem_limit_bytes=60 * 1024 * 1024
         ),
-    )(counts, re, ce, rm, cm)
-    return adagrad(re, ra, gr), adagrad(ce, ca, gc)
+    )(counts, re, ce, rm, cm, ra, ca)
+    return re - gr, ce - gc
 
 
 def solution(mesh):

time: 55.8 us -> 56.1 us (level)
  other arithmetic: 1.72 us -> 3.15 us
  Pallas kernels: 52.5 us -> 51.9 us
    sub x1 -> x2, other arithmetic: 1.72 us -> 3.15 us  [local(): return (re - gr, ce - gc)]
where the time goes in v7:
time: 56.1 us; the launch traced here: 55.7 us
  Pallas kernels  51.9 us (93%)
  other arithmetic  3.15 us (6%)
  between operations  0.66 us (1%)
    pallas_call x1, Pallas kernels, local(): pl.pallas_call(functools.partial(kernel, NZ, XN, B, D, CB), out_shape=(ja...  51.9 us
    sub x2, other arithmetic, local(): return (re - gr, ce - gc)  3.15 us

profile of v7, /device:TPU:8, one launch (start us, length us, event | category | flops | bytes accessed | tf_op | source)
XLA Modules:
  0.0 55.7 jit_solution(18047598379691552463)
XLA Ops:
  0.6 0.0 copy-start.1
  0.6 0.0 copy-start
  0.7 51.9 %shard_map.86 = (f32[2,64,256]{2,1,0:T(8,128)}, f32[2,64,256]{2,1,0:T(8,128)}) custom-call(s32[2,8,256,512]{3,2,1,0:T(8,128)} %bitcast.1, f32[2,64,256]{2,1,0:T(8,128)} %re_h.1, f32[2,64,256]{2,1,0:T(8,128)} %ce_h.1, s32[2,64]{1,0:T(2,128)} %rm_h.1, s32[2,64]{1,0:T(2,128)} %cm_h.1, f32[2,64,256]{2,1,0:T(8,128)} %ra_h.1, f32[2,64,256]{2,1,0:T(8,128)} %ca_h.1), custom_call_target="tpu_custom_call" | custom-call | tf_op jit(solution)/shard_map/pallas_call | solution.py:519
  52.6 0.0 copy-done
  52.6 1.6 %sub.6 = f32[2,64,256]{2,1,0:T(8,128)} subtract(f32[2,64,256]{2,1,0:T(8,128)S(1)} %copy-done, f32[2,64,256]{2,1,0:T(8,128)} %get-tuple-element.4) | non-fusion elementwise | flops 32768 | bytes 393216 | tf_op jit(solution)/shard_map/sub | solution.py:529
  54.1 0.0 copy-done.1
  54.1 1.6 %sub.7 = f32[2,64,256]{2,1,0:T(8,128)} subtract(f32[2,64,256]{2,1,0:T(8,128)S(1)} %copy-done.1, f32[2,64,256]{2,1,0:T(8,128)} %get-tuple-element.5) | non-fusion elementwise | flops 32768 | bytes 393216 | tf_op jit(solution)/shard_map/sub | solution.py:529
Async XLA Ops:
  0.6 53.5 %copy-start.1 = (f32[2,64,256]{2,1,0:T(8,128)S(1)}, f32[2,64,256]{2,1,0:T(8,128)}, u32[]{:S(2)}) copy-start(f32[2,64,256]{2,1,0:T(8,128)} %ce_h.1) | copy-start | bytes 393220
  0.6 51.9 %copy-start = (f32[2,64,256]{2,1,0:T(8,128)S(1)}, f32[2,64,256]{2,1,0:T(8,128)}, u32[]{:S(2)}) copy-start(f32[2,64,256]{2,1,0:T(8,128)} %re_h.1) | copy-start | bytes 393220

commit v8 on v7

--- a/solution.py
+++ b/solution.py
@@ -19,15 +19,15 @@
     return lax.dot_general(a, b, dims, preferred_element_type=F32)
 
 
-def update(g, a):
-    return g / jnp.sqrt(a + g * g)
+def adagrad(w, a, g):
+    return w - g / jnp.sqrt(a + g * g)
 
 
 def kernel(
     NZ, XN, B, D, CN,
-    counts, re_h, ce_h, rm_h, cm_h, ra_h, ca_h, nr, nc,
-    re, ce, rm, cm, ra, ca,
-    cnt, rows, cols, colsT, colsC, LRB, LC, PA, PB, RP, CPT, CP,
+    counts, re_h, ce_h, rm_h, cm_h, nr, nc,
+    re, ce, rm, cm,
+    cnt, rows, cols, colsT, colsC, LRB, LC, RP, CPT, CP,
     CS, CR, RSp, RSm, RRp, RRm, YS, YR, VR, Q1s, Q1r, Q2s, Q2r, Q3s, Q3r, VC, gr, gc,
     s_in, s_cnt, s_all, s_out, r_row, r_core, r_col, r_cr, r_rp, r_rm, r_y, r_q,
 ):
@@ -83,7 +83,7 @@
 
     own_in = [
         pltpu.make_async_copy(src, dst, s_in.at[i])
-        for i, (src, dst) in enumerate(((rm_h, rm), (cm_h, cm), (re_h, re), (ce_h, ce), (ra_h, ra), (ca_h, ca)))
+        for i, (src, dst) in enumerate(((rm_h, rm), (cm_h, cm), (re_h, re), (ce_h, ce)))
     ]
     for copy in own_in:
         copy.start()
@@ -109,11 +109,13 @@
         at = pl.ds(pl.multiple_of(q * 4 * B, 4 * B), 4 * B)
         return pltpu.make_async_copy(counts.at[q // NZ, zc], cnt.at[at], s_cnt.at[q])
 
-    AHEAD = 3
-    for u in range(AHEAD):
-        count_copy(u).start()
-
-    for copy in own_in[:4]:
+    def counts_out(lo, hi):
+        for u in range(lo, hi):
+            count_copy(u).start()
+
+    counts_out(0, 3)
+
+    for copy in own_in:
         copy.wait()
 
     def own_block(embed, margs, shift):
@@ -194,28 +196,6 @@
         arrive(col_block(s, yl, x2), r_col.at[s, 3])
         arrive(col_block(s, 1 - yl, x2), r_col.at[s, 4])
 
-    def preps(lo, hi):
-        def chunk(u, carry):
-            @pl.when(u + AHEAD < NS * NZ)
-            def _():
-                count_copy(u + AHEAD).start()
-
-            count_copy(u).wait()
-            q = in_turn(u)
-
-            def part(i, carry):
-                at = pl.ds(pl.multiple_of(i * 128, 128), 128)
-                n = cnt[pl.ds(pl.multiple_of(q * 4 * B + i * 128, 128), 128), :].astype(F32)
-                m = jnp.maximum(n, 1.0)
-                conf = jnp.where(n > 0, 0.4 + m * lax.rsqrt(m), 0.0)
-                PA[q, at, :] = conf
-                PB[q, at, :] = 0.5 * conf * jnp.log(m)
-                return carry
-
-            return lax.fori_loop(0, 4 * B // 128, part, carry)
-
-        lax.fori_loop(lo, hi, chunk, 0)
-
     def halves(s, a, b):
         return jnp.concatenate([a[:, s * B : (s + 1) * B], b[:, s * B : (s + 1) * B]], axis=1)
 
@@ -244,9 +224,10 @@
         left = rows[pair, :, :, pl.ds(pl.multiple_of(s * (B + 16), 16), B), :].reshape(8 * B, D)
         lr = LRB[s, pair].reshape(8 * B, 128)
         t = dot(left, colsT[s], NN) + jnp.concatenate([lr] * (CN // 128), axis=1) + LC[s]
-        conf = PA[pl.ds(s * NZ + p, 2)].reshape(8 * B, CN)
-        plain = PB[pl.ds(s * NZ + p, 2)].reshape(8 * B, CN)
-        g = jnp.where(conf > 0, conf * t - plain, jnp.tanh(t) + 1.0).astype(BF16)
+        n = cnt[pl.ds(pl.multiple_of((s * NZ + p) * 4 * B, 8 * B), 8 * B), :].astype(F32)
+        m = jnp.maximum(n, 1.0)
+        there = (0.4 + m * lax.rsqrt(m)) * (t - 0.5 * jnp.log(m))
+        g = jnp.where(n > 0, there, jnp.tanh(t) + 1.0).astype(BF16)
         RP[s, pair] = dot(g, colsC[s], NN).reshape(2, 2, 2, B, D)
         CS[s, pair] = RP[s, pair, :, oc].astype(BF16)
         CPT[s] += dot(left.T, g, NN)
@@ -313,7 +294,7 @@
 
     def rows_out(s):
         arrive(YR.at[s], r_y.at[s])
-        gr[s] = update(0.5 * (VR[s] + YR[s].astype(F32)), ra[s])
+        gr[s] = 0.5 * (VR[s] + YR[s].astype(F32))
         out_copy(0, s).start()
 
     def col_far(s):
@@ -342,7 +323,7 @@
 
     def cols_out(s):
         arrive(Q3r.at[s], r_q.at[s, 4])
-        gc[s] = update(0.5 * (VC[s] + Q3r[s].astype(F32)), ca[s])
+        gc[s] = 0.5 * (VC[s] + Q3r[s].astype(F32))
         out_copy(1, s).start()
 
     for s in range(NS):
@@ -350,39 +331,37 @@
         send(row_block(s, 0, 0), row_block(s, 0, 0), r_row.at[s, 0, 1], to_yh, s)
         send_row(s, 0, 0, True)
         send_row(s, 0, 0, False)
-    preps(0, 1)
     col_y(0)
     row_step(0, 0, 1)
     row_y(0)
     row_step(1, 0, 1)
     col_y(1)
-    preps(1, 2)
+    counts_out(3, 6)
     row_step(0, 0, 2)
     col_x(0)
     row_y(1)
     row_step(1, 0, 2)
-    preps(2, 3)
     row_step(0, 1, 1)
     row_core(0, 0)
     col_x(1)
+    counts_out(6, 9)
     row_step(0, 0, 3)
-    preps(3, 4)
     row_step(1, 1, 1)
     row_core(1, 0)
     row_step(1, 0, 3)
-    preps(4, 5)
     all_cols(0)
     col_lines()
     turn(0)
+    counts_out(9, 12)
     row_step(0, 1, 2)
     row_core(0, 1)
-    preps(5, 6)
 
     def before(i):
         if i == 0:
             core_here(0, 0)
             lift(0)
         if i == 1:
+            counts_out(12, 16)
             far_out(0)
             row_step(1, 1, 2)
             row_core(1, 1)
@@ -400,26 +379,21 @@
             row_core(1, 2)
             row_here(0, 1, H)
             row_core(0, 3)
-            preps(6, 8)
             core_here(0, 2)
             lift(4)
         if i == 4:
             row_here(1, 1, H)
             row_core(1, 3)
-            preps(8, 10)
             core_here(0, 3)
             lift(6)
         if i == 5:
-            preps(10, 12)
             core_here(1, 3)
         if i == 6:
             ring(0, H)
-            preps(12, 14)
             core_here(1, 2)
         if i == 7:
             ring(1, H)
             col_far(0)
-            preps(14, 16)
             ring(0, 3)
             core_here(1, 1)
 
@@ -428,14 +402,14 @@
             pl.when(i == k)(functools.partial(before, k))
         s, j = turn_of(i)
         p = 2 * j
+        count_copy(2 * i).wait()
+        count_copy(2 * i + 1).wait()
         unit(s, p)
         part = pl.ds(p, 2)
         send(CS.at[s, part], CR.at[s, part], r_cr.at[s, j], to_core, 1, 4 * 2 * H)
         return carry
 
     lax.fori_loop(0, 2 * H, step, 0)
-    for copy in own_in[4:]:
-        copy.wait()
     ring(1, 3)
     col_near(0)
     ring(0, 2)
@@ -471,8 +445,6 @@
         v((S, B, D), F32),
         v((S, B), jnp.int32),
         v((S, B), jnp.int32),
-        v((S, B, D), F32),
-        v((S, B, D), F32),
         v((S * NZ * 4 * B, CB), jnp.int32),
         v((NZ, 2, 2, 2 * B + 16, D), BF16),
         v((2, XN, 2 * B + 16, D), BF16),
@@ -480,8 +452,6 @@
         v((S, CB, D), BF16),
         v((S, NZ, 4 * B, 128), F32),
         v((S, 1, CB), F32),
-        v((S * NZ, 4 * B, CB), F32),
-        v((S * NZ, 4 * B, CB), F32),
         v((S, NZ, 2, 2, B, D), F32),
         v((S, D, CB), F32),
         v((S, R, B, D), F32),
@@ -503,7 +473,7 @@
         v((S, B, D), F32),
         v((S, B, D), F32),
         v((S, B, D), F32),
-        sem((6,)),
+        sem((4,)),
         sem((S * NZ,)),
         sem(()),
         sem((2, S)),
@@ -519,14 +489,14 @@
     gr, gc = pl.pallas_call(
         functools.partial(kernel, NZ, XN, B, D, CB),
         out_shape=(jax.ShapeDtypeStruct((S, B, D), F32), jax.ShapeDtypeStruct((S, B, D), F32)),
-        in_specs=[pl.BlockSpec(memory_space=pltpu.HBM)] * 7,
+        in_specs=[pl.BlockSpec(memory_space=pltpu.HBM)] * 5,
         out_specs=(pl.BlockSpec(memory_space=pltpu.HBM),) * 2,
         scratch_shapes=scratch,
         compiler_params=pltpu.CompilerParams(
             collective_id=0, has_side_effects=True, vmem_limit_bytes=60 * 1024 * 1024
         ),
-    )(counts, re, ce, rm, cm, ra, ca)
-    return re - gr, ce - gc
+    )(counts, re, ce, rm, cm)
+    return adagrad(re, ra, gr), adagrad(ce, ca, gc)
 
 
 def solution(mesh):

time: 56.1 us -> 53.9 us (0.961)
  other arithmetic: 3.15 us -> 1.72 us
    sub x2 -> x1, other arithmetic: 3.15 us -> 1.72 us  [adagrad(): return w - g / jnp.sqrt(a + g * g)]
where the time goes in v8:
time: 53.9 us; the launch traced here: 53.8 us
  Pallas kernels  51.4 us (95%)
  other arithmetic  1.72 us (3%)
  between operations  0.7 us (1%)
    pallas_call x1, Pallas kernels, local(): pl.pallas_call(functools.partial(kernel, NZ, XN, B, D, CB), out_shape=(ja...  51.4 us
    sub x1, other arithmetic, adagrad(): return w - g / jnp.sqrt(a + g * g)  1.72 us

profile of v8, /device:TPU:8, one launch (start us, length us, event | category | flops | bytes accessed | tf_op | source)
XLA Modules:
  0.0 53.8 jit_solution(12009347758012676830)
XLA Ops:
  0.6 0.0 copy-start
  0.6 0.0 copy-start.1
  0.7 0.0 copy-start.2
  0.7 0.0 copy-start.3
  0.7 51.4 %shard_map.86 = (f32[2,64,256]{2,1,0:T(8,128)}, f32[2,64,256]{2,1,0:T(8,128)}) custom-call(s32[2,8,256,512]{3,2,1,0:T(8,128)} %bitcast.1, f32[2,64,256]{2,1,0:T(8,128)} %re_h.1, f32[2,64,256]{2,1,0:T(8,128)} %ce_h.1, s32[2,64]{1,0:T(2,128)} %rm_h.1, s32[2,64]{1,0:T(2,128)} %cm_h.1), custom_call_target="tpu_custom_call" | custom-call | tf_op jit(solution)/shard_map/pallas_call | solution.py:489
  52.1 0.0 copy-done
  52.1 0.0 copy-done.1
  52.1 0.0 copy-done.2
  52.1 0.0 copy-done.3
  52.1 1.7 %multiply_subtract_fusion = (f32[2,64,256]{2,1,0:T(8,128)}, f32[2,64,256]{2,1,0:T(8,128)}) fusion(f32[2,64,256]{2,1,0:T(8,128)S(1)} %copy-done, f32[2,64,256]{2,1,0:T(8,128)} %get-tuple-element.5, f32[2,64,256]{2,1,0:T(8,128)S(1)} %copy-done.2, f32[2,64,256]{2,1,0:T(8,128)S(1)} %copy-done.1, f32[2,64,256]{2,1,0:T(8,128)} %get-tuple-element.4, ...), kind=kLoop, calls=%fused_computation | loop fusion | flops 262144 | bytes 1048576 | tf_op jit(solution)/shard_map/sub | solution.py:23
Async XLA Ops:
  0.6 51.4 %copy-start = (f32[2,64,256]{2,1,0:T(8,128)S(1)}, f32[2,64,256]{2,1,0:T(8,128)}, u32[]{:S(2)}) copy-start(f32[2,64,256]{2,1,0:T(8,128)} %ce_h.1) | copy-start | bytes 393220
  0.6 51.4 %copy-start.1 = (f32[2,64,256]{2,1,0:T(8,128)S(1)}, f32[2,64,256]{2,1,0:T(8,128)}, u32[]{:S(2)}) copy-start(f32[2,64,256]{2,1,0:T(8,128)} %re_h.1) | copy-start | bytes 393220
  0.7 51.4 %copy-start.2 = (f32[2,64,256]{2,1,0:T(8,128)S(1)}, f32[2,64,256]{2,1,0:T(8,128)}, u32[]{:S(2)}) copy-start(f32[2,64,256]{2,1,0:T(8,128)} %param.13) | copy-start | bytes 393220
  0.7 51.4 %copy-start.3 = (f32[2,64,256]{2,1,0:T(8,128)S(1)}, f32[2,64,256]{2,1,0:T(8,128)}, u32[]{:S(2)}) copy-start(f32[2,64,256]{2,1,0:T(8,128)} %param.12) | copy-start | bytes 393220

commit v9 on v8

--- a/solution.py
+++ b/solution.py
@@ -94,8 +94,8 @@
         pl.semaphore_signal(barrier, inc=1, device_id=dev, device_id_type=MESH)
 
     def turn_of(i):
-        first, second, late = (i + 7) // 8, (i + 6) // 8, (i + 3) // 8
-        return late + first - second, (1 - late) * (i - first) + late * (8 - i)
+        s = i // H
+        return s, i * (1 - s) + (2 * H - 1 - i) * s
 
     def in_turn(u):
         s, j = turn_of(u // 2)
@@ -226,7 +226,8 @@
         t = dot(left, colsT[s], NN) + jnp.concatenate([lr] * (CN // 128), axis=1) + LC[s]
         n = cnt[pl.ds(pl.multiple_of((s * NZ + p) * 4 * B, 8 * B), 8 * B), :].astype(F32)
         m = jnp.maximum(n, 1.0)
-        there = (0.4 + m * lax.rsqrt(m)) * (t - 0.5 * jnp.log(m))
+        root = m * lax.rsqrt(m)
+        there = (0.4 + root) * (t - jnp.log(root))
         g = jnp.where(n > 0, there, jnp.tanh(t) + 1.0).astype(BF16)
         RP[s, pair] = dot(g, colsC[s], NN).reshape(2, 2, 2, B, D)
         CS[s, pair] = RP[s, pair, :, oc].astype(BF16)
@@ -365,37 +366,40 @@
             far_out(0)
             row_step(1, 1, 2)
             row_core(1, 1)
-            all_cols(1)
-            turn(1)
-            core_here(1, 0)
-        if i == 2:
             row_step(0, 1, 3)
             row_core(0, 2)
             far_out(1)
             core_here(0, 1)
             lift(2)
-        if i == 3:
+        if i == 2:
+            row_here(0, 1, H)
+            row_core(0, 3)
             row_step(1, 1, 3)
             row_core(1, 2)
-            row_here(0, 1, H)
-            row_core(0, 3)
             core_here(0, 2)
             lift(4)
-        if i == 4:
+        if i == 3:
             row_here(1, 1, H)
             row_core(1, 3)
             core_here(0, 3)
             lift(6)
+        if i == 4:
+            all_cols(1)
+            turn(1)
+            core_here(1, 3)
         if i == 5:
-            core_here(1, 3)
-        if i == 6:
             ring(0, H)
             core_here(1, 2)
-        if i == 7:
+        if i == 6:
             ring(1, H)
             col_far(0)
             ring(0, 3)
             core_here(1, 1)
+        if i == 7:
+            ring(1, 3)
+            col_near(0)
+            ring(0, 2)
+            core_here(1, 0)
 
     def step(i, carry):
         for k in range(2 * H):
@@ -410,19 +414,16 @@
         return carry
 
     lax.fori_loop(0, 2 * H, step, 0)
-    ring(1, 3)
-    col_near(0)
-    ring(0, 2)
     col_far(1)
     ring(1, 2)
     col_own(0)
     ring(0, 1)
+    ring(1, 1)
     col_near(1)
-    ring(1, 1)
     cols_out(0)
     ring(0, 0)
+    ring(1, 0)
     col_own(1)
-    ring(1, 0)
     rows_out(0)
     cols_out(1)
     rows_out(1)

time: 53.9 us -> 55.6 us (1.032)
  Pallas kernels: 51.4 us -> 53 us
    pallas_call x1, Pallas kernels: 51.4 us -> 53 us  [local(): pl.pallas_call(functools.partial(kernel, NZ, XN, B, D, CB), out_shape=(ja...]
where the time goes in v9:
time: 55.6 us; the launch traced here: 55.5 us
  Pallas kernels  53 us (95%)
  other arithmetic  1.72 us (3%)
  between operations  0.7 us (1%)
    pallas_call x1, Pallas kernels, local(): pl.pallas_call(functools.partial(kernel, NZ, XN, B, D, CB), out_shape=(ja...  53 us
    sub x1, other arithmetic, adagrad(): return w - g / jnp.sqrt(a + g * g)  1.72 us

profile of v9, /device:TPU:8, one launch (start us, length us, event | category | flops | bytes accessed | tf_op | source)
XLA Modules:
  0.0 55.5 jit_solution(8837147441462915695)
XLA Ops:
  0.6 0.0 copy-start
  0.6 0.0 copy-start.1
  0.7 0.0 copy-start.2
  0.7 0.0 copy-start.3
  0.7 53.0 %shard_map.86 = (f32[2,64,256]{2,1,0:T(8,128)}, f32[2,64,256]{2,1,0:T(8,128)}) custom-call(s32[2,8,256,512]{3,2,1,0:T(8,128)} %bitcast.1, f32[2,64,256]{2,1,0:T(8,128)} %re_h.1, f32[2,64,256]{2,1,0:T(8,128)} %ce_h.1, s32[2,64]{1,0:T(2,128)} %rm_h.1, s32[2,64]{1,0:T(2,128)} %cm_h.1), custom_call_target="tpu_custom_call" | custom-call | tf_op jit(solution)/shard_map/pallas_call | solution.py:490
  53.7 0.0 copy-done
  53.7 0.0 copy-done.1
  53.7 0.0 copy-done.2
  53.8 0.0 copy-done.3
  53.8 1.7 %multiply_subtract_fusion = (f32[2,64,256]{2,1,0:T(8,128)}, f32[2,64,256]{2,1,0:T(8,128)}) fusion(f32[2,64,256]{2,1,0:T(8,128)S(1)} %copy-done, f32[2,64,256]{2,1,0:T(8,128)} %get-tuple-element.5, f32[2,64,256]{2,1,0:T(8,128)S(1)} %copy-done.2, f32[2,64,256]{2,1,0:T(8,128)S(1)} %copy-done.1, f32[2,64,256]{2,1,0:T(8,128)} %get-tuple-element.4, ...), kind=kLoop, calls=%fused_computation | loop fusion | flops 262144 | bytes 1048576 | tf_op jit(solution)/shard_map/sub | solution.py:23
Async XLA Ops:
  0.6 53.1 %copy-start = (f32[2,64,256]{2,1,0:T(8,128)S(1)}, f32[2,64,256]{2,1,0:T(8,128)}, u32[]{:S(2)}) copy-start(f32[2,64,256]{2,1,0:T(8,128)} %ce_h.1) | copy-start | bytes 393220
  0.6 53.1 %copy-start.1 = (f32[2,64,256]{2,1,0:T(8,128)S(1)}, f32[2,64,256]{2,1,0:T(8,128)}, u32[]{:S(2)}) copy-start(f32[2,64,256]{2,1,0:T(8,128)} %re_h.1) | copy-start | bytes 393220
  0.7 53.1 %copy-start.2 = (f32[2,64,256]{2,1,0:T(8,128)S(1)}, f32[2,64,256]{2,1,0:T(8,128)}, u32[]{:S(2)}) copy-start(f32[2,64,256]{2,1,0:T(8,128)} %param.13) | copy-start | bytes 393220
  0.7 53.1 %copy-start.3 = (f32[2,64,256]{2,1,0:T(8,128)S(1)}, f32[2,64,256]{2,1,0:T(8,128)}, u32[]{:S(2)}) copy-start(f32[2,64,256]{2,1,0:T(8,128)} %param.12) | copy-start | bytes 393220

commit v10 on v8

--- a/solution.py
+++ b/solution.py
@@ -220,17 +220,20 @@
         CPT[s] = jnp.zeros_like(CPT[s])
 
     def unit(s, p):
-        pair = pl.ds(p, 2)
-        left = rows[pair, :, :, pl.ds(pl.multiple_of(s * (B + 16), 16), B), :].reshape(8 * B, D)
-        lr = LRB[s, pair].reshape(8 * B, 128)
-        t = dot(left, colsT[s], NN) + jnp.concatenate([lr] * (CN // 128), axis=1) + LC[s]
-        n = cnt[pl.ds(pl.multiple_of((s * NZ + p) * 4 * B, 8 * B), 8 * B), :].astype(F32)
-        m = jnp.maximum(n, 1.0)
-        there = (0.4 + m * lax.rsqrt(m)) * (t - 0.5 * jnp.log(m))
-        g = jnp.where(n > 0, there, jnp.tanh(t) + 1.0).astype(BF16)
-        RP[s, pair] = dot(g, colsC[s], NN).reshape(2, 2, 2, B, D)
-        CS[s, pair] = RP[s, pair, :, oc].astype(BF16)
-        CPT[s] += dot(left.T, g, NN)
+        lefts, grads = [], []
+        for q in range(2):
+            left = rows[p + q, :, :, pl.ds(pl.multiple_of(s * (B + 16), 16), B), :].reshape(4 * B, D)
+            t = dot(left, colsT[s], NN) + jnp.concatenate([LRB[s, p + q]] * (CN // 128), axis=1) + LC[s]
+            n = cnt[pl.ds(pl.multiple_of((s * NZ + p + q) * 4 * B, 4 * B), 4 * B), :].astype(F32)
+            m = jnp.maximum(n, 1.0)
+            root = m * lax.rsqrt(m)
+            there = (0.4 + root) * (t - jnp.log(root))
+            g = jnp.where(n > 0, there, jnp.tanh(t) + 1.0).astype(BF16)
+            RP[s, p + q] = dot(g, colsC[s], NN).reshape(2, 2, B, D)
+            CS[s, p + q] = RP[s, p + q, :, oc].astype(BF16)
+            lefts.append(left)
+            grads.append(g)
+        CPT[s] += dot(jnp.concatenate(lefts, axis=0).T, jnp.concatenate(grads, axis=0), NN)
 
     def sums_here(s, j):
         arrive(CR.at[s, pl.ds(2 * j, 2)], r_cr.at[s, j])

time: 53.9 us -> 54 us (level)
  no operation moved by 1% of the time
where the time goes in v10:
time: 54 us; the launch traced here: 53.9 us
  Pallas kernels  51.5 us (95%)
  other arithmetic  1.72 us (3%)
  between operations  0.7 us (1%)
    pallas_call x1, Pallas kernels, local(): pl.pallas_call(functools.partial(kernel, NZ, XN, B, D, CB), out_shape=(ja...  51.5 us
    sub x1, other arithmetic, adagrad(): return w - g / jnp.sqrt(a + g * g)  1.72 us

profile of v10, /device:TPU:8, one launch (start us, length us, event | category | flops | bytes accessed | tf_op | source)
XLA Modules:
  0.0 53.9 jit_solution(7190252627091688918)
XLA Ops:
  0.6 0.0 copy-start
  0.6 0.0 copy-start.1
  0.7 0.0 copy-start.2
  0.7 0.0 copy-start.3
  0.7 51.5 %shard_map.86 = (f32[2,64,256]{2,1,0:T(8,128)}, f32[2,64,256]{2,1,0:T(8,128)}) custom-call(s32[2,8,256,512]{3,2,1,0:T(8,128)} %bitcast.1, f32[2,64,256]{2,1,0:T(8,128)} %re_h.1, f32[2,64,256]{2,1,0:T(8,128)} %ce_h.1, s32[2,64]{1,0:T(2,128)} %rm_h.1, s32[2,64]{1,0:T(2,128)} %cm_h.1), custom_call_target="tpu_custom_call" | custom-call | tf_op jit(solution)/shard_map/pallas_call | solution.py:492
  52.2 0.0 copy-done
  52.2 0.0 copy-done.1
  52.2 0.0 copy-done.2
  52.2 0.0 copy-done.3
  52.2 1.7 %multiply_subtract_fusion = (f32[2,64,256]{2,1,0:T(8,128)}, f32[2,64,256]{2,1,0:T(8,128)}) fusion(f32[2,64,256]{2,1,0:T(8,128)S(1)} %copy-done, f32[2,64,256]{2,1,0:T(8,128)} %get-tuple-element.5, f32[2,64,256]{2,1,0:T(8,128)S(1)} %copy-done.2, f32[2,64,256]{2,1,0:T(8,128)S(1)} %copy-done.1, f32[2,64,256]{2,1,0:T(8,128)} %get-tuple-element.4, ...), kind=kLoop, calls=%fused_computation | loop fusion | flops 262144 | bytes 1048576 | tf_op jit(solution)/shard_map/sub | solution.py:23
Async XLA Ops:
  0.6 51.5 %copy-start = (f32[2,64,256]{2,1,0:T(8,128)S(1)}, f32[2,64,256]{2,1,0:T(8,128)}, u32[]{:S(2)}) copy-start(f32[2,64,256]{2,1,0:T(8,128)} %ce_h.1) | copy-start | bytes 393220
  0.6 51.5 %copy-start.1 = (f32[2,64,256]{2,1,0:T(8,128)S(1)}, f32[2,64,256]{2,1,0:T(8,128)}, u32[]{:S(2)}) copy-start(f32[2,64,256]{2,1,0:T(8,128)} %re_h.1) | copy-start | bytes 393220
  0.7 51.5 %copy-start.2 = (f32[2,64,256]{2,1,0:T(8,128)S(1)}, f32[2,64,256]{2,1,0:T(8,128)}, u32[]{:S(2)}) copy-start(f32[2,64,256]{2,1,0:T(8,128)} %param.13) | copy-start | bytes 393220
  0.7 51.5 %copy-start.3 = (f32[2,64,256]{2,1,0:T(8,128)S(1)}, f32[2,64,256]{2,1,0:T(8,128)}, u32[]{:S(2)}) copy-start(f32[2,64,256]{2,1,0:T(8,128)} %param.12) | copy-start | bytes 393220

commit v11 on v9

--- a/solution.py
+++ b/solution.py
@@ -113,7 +113,7 @@
         for u in range(lo, hi):
             count_copy(u).start()
 
-    counts_out(0, 3)
+    counts_out(0, 4)
 
     for copy in own_in:
         copy.wait()
@@ -337,7 +337,6 @@
     row_y(0)
     row_step(1, 0, 1)
     col_y(1)
-    counts_out(3, 6)
     row_step(0, 0, 2)
     col_x(0)
     row_y(1)
@@ -345,7 +344,6 @@
     row_step(0, 1, 1)
     row_core(0, 0)
     col_x(1)
-    counts_out(6, 9)
     row_step(0, 0, 3)
     row_step(1, 1, 1)
     row_core(1, 0)
@@ -353,22 +351,22 @@
     all_cols(0)
     col_lines()
     turn(0)
-    counts_out(9, 12)
     row_step(0, 1, 2)
     row_core(0, 1)
+    far_out(0)
 
     def before(i):
+        if i > 0:
+            counts_out(2 * i + 2, min(2 * i + 4, NS * NZ))
         if i == 0:
             core_here(0, 0)
             lift(0)
         if i == 1:
-            counts_out(12, 16)
-            far_out(0)
             row_step(1, 1, 2)
             row_core(1, 1)
+            far_out(1)
             row_step(0, 1, 3)
             row_core(0, 2)
-            far_out(1)
             core_here(0, 1)
             lift(2)
         if i == 2:

time: 55.6 us -> 54.9 us (0.987)
  Pallas kernels: 53 us -> 52.4 us
    pallas_call x1, Pallas kernels: 53 us -> 52.4 us  [local(): pl.pallas_call(functools.partial(kernel, NZ, XN, B, D, CB), out_shape=(ja...]
where the time goes in v11:
time: 54.9 us; the launch traced here: 54.8 us
  Pallas kernels  52.4 us (95%)
  other arithmetic  1.72 us (3%)
  between operations  0.7 us (1%)
    pallas_call x1, Pallas kernels, local(): pl.pallas_call(functools.partial(kernel, NZ, XN, B, D, CB), out_shape=(ja...  52.4 us
    sub x1, other arithmetic, adagrad(): return w - g / jnp.sqrt(a + g * g)  1.72 us

profile of v11, /device:TPU:8, one launch (start us, length us, event | category | flops | bytes accessed | tf_op | source)
XLA Modules:
  0.0 54.8 jit_solution(4535345890071338012)
XLA Ops:
  0.6 0.0 copy-start
  0.6 0.0 copy-start.1
  0.7 0.0 copy-start.2
  0.7 0.0 copy-start.3
  0.7 52.4 %shard_map.86 = (f32[2,64,256]{2,1,0:T(8,128)}, f32[2,64,256]{2,1,0:T(8,128)}) custom-call(s32[2,8,256,512]{3,2,1,0:T(8,128)} %bitcast.1, f32[2,64,256]{2,1,0:T(8,128)} %re_h.1, f32[2,64,256]{2,1,0:T(8,128)} %ce_h.1, s32[2,64]{1,0:T(2,128)} %rm_h.1, s32[2,64]{1,0:T(2,128)} %cm_h.1), custom_call_target="tpu_custom_call" | custom-call | tf_op jit(solution)/shard_map/pallas_call | solution.py:488
  53.0 0.0 copy-done
  53.0 0.0 copy-done.1
  53.1 0.0 copy-done.2
  53.1 0.0 copy-done.3
  53.1 1.7 %multiply_subtract_fusion = (f32[2,64,256]{2,1,0:T(8,128)}, f32[2,64,256]{2,1,0:T(8,128)}) fusion(f32[2,64,256]{2,1,0:T(8,128)S(1)} %copy-done, f32[2,64,256]{2,1,0:T(8,128)} %get-tuple-element.5, f32[2,64,256]{2,1,0:T(8,128)S(1)} %copy-done.2, f32[2,64,256]{2,1,0:T(8,128)S(1)} %copy-done.1, f32[2,64,256]{2,1,0:T(8,128)} %get-tuple-element.4, ...), kind=kLoop, calls=%fused_computation | loop fusion | flops 262144 | bytes 1048576 | tf_op jit(solution)/shard_map/sub | solution.py:23
Async XLA Ops:
  0.6 52.4 %copy-start = (f32[2,64,256]{2,1,0:T(8,128)S(1)}, f32[2,64,256]{2,1,0:T(8,128)}, u32[]{:S(2)}) copy-start(f32[2,64,256]{2,1,0:T(8,128)} %ce_h.1) | copy-start | bytes 393220
  0.6 52.4 %copy-start.1 = (f32[2,64,256]{2,1,0:T(8,128)S(1)}, f32[2,64,256]{2,1,0:T(8,128)}, u32[]{:S(2)}) copy-start(f32[2,64,256]{2,1,0:T(8,128)} %re_h.1) | copy-start | bytes 393220
  0.7 52.4 %copy-start.2 = (f32[2,64,256]{2,1,0:T(8,128)S(1)}, f32[2,64,256]{2,1,0:T(8,128)}, u32[]{:S(2)}) copy-start(f32[2,64,256]{2,1,0:T(8,128)} %param.13) | copy-start | bytes 393220
  0.7 52.4 %copy-start.3 = (f32[2,64,256]{2,1,0:T(8,128)S(1)}, f32[2,64,256]{2,1,0:T(8,128)}, u32[]{:S(2)}) copy-start(f32[2,64,256]{2,1,0:T(8,128)} %param.12) | copy-start | bytes 393220

commit v12 on v8

--- a/solution.py
+++ b/solution.py
@@ -226,7 +226,8 @@
         t = dot(left, colsT[s], NN) + jnp.concatenate([lr] * (CN // 128), axis=1) + LC[s]
         n = cnt[pl.ds(pl.multiple_of((s * NZ + p) * 4 * B, 8 * B), 8 * B), :].astype(F32)
         m = jnp.maximum(n, 1.0)
-        there = (0.4 + m * lax.rsqrt(m)) * (t - 0.5 * jnp.log(m))
+        root = m * lax.rsqrt(m)
+        there = (0.4 + root) * (t - jnp.log(root))
         g = jnp.where(n > 0, there, jnp.tanh(t) + 1.0).astype(BF16)
         RP[s, pair] = dot(g, colsC[s], NN).reshape(2, 2, 2, B, D)
         CS[s, pair] = RP[s, pair, :, oc].astype(BF16)
@@ -331,30 +332,33 @@
         send(row_block(s, 0, 0), row_block(s, 0, 0), r_row.at[s, 0, 1], to_yh, s)
         send_row(s, 0, 0, True)
         send_row(s, 0, 0, False)
+    row_step(0, 0, 1)
     col_y(0)
-    row_step(0, 0, 1)
     row_y(0)
     row_step(1, 0, 1)
     col_y(1)
     counts_out(3, 6)
     row_step(0, 0, 2)
-    col_x(0)
     row_y(1)
     row_step(1, 0, 2)
     row_step(0, 1, 1)
     row_core(0, 0)
-    col_x(1)
+    col_x(0)
     counts_out(6, 9)
     row_step(0, 0, 3)
     row_step(1, 1, 1)
     row_core(1, 0)
+    col_x(1)
     row_step(1, 0, 3)
+    row_step(0, 1, 2)
+    row_core(0, 1)
+    counts_out(9, 12)
+    far_out(0)
+    row_step(1, 1, 2)
+    row_core(1, 1)
     all_cols(0)
     col_lines()
     turn(0)
-    counts_out(9, 12)
-    row_step(0, 1, 2)
-    row_core(0, 1)
 
     def before(i):
         if i == 0:
@@ -362,16 +366,13 @@
             lift(0)
         if i == 1:
             counts_out(12, 16)
-            far_out(0)
-            row_step(1, 1, 2)
-            row_core(1, 1)
+            far_out(1)
             all_cols(1)
             turn(1)
             core_here(1, 0)
         if i == 2:
             row_step(0, 1, 3)
             row_core(0, 2)
-            far_out(1)
             core_here(0, 1)
             lift(2)
         if i == 3:

time: 53.9 us -> 53.7 us (level)
  Pallas kernels: 51.4 us -> 50.8 us
where the time goes in v12:
time: 53.7 us; the launch traced here: 53.3 us
  Pallas kernels  50.8 us (95%)
  other arithmetic  1.72 us (3%)
  between operations  0.7 us (1%)
    pallas_call x1, Pallas kernels, local(): pl.pallas_call(functools.partial(kernel, NZ, XN, B, D, CB), out_shape=(ja...  50.8 us
    sub x1, other arithmetic, adagrad(): return w - g / jnp.sqrt(a + g * g)  1.72 us

profile of v12, /device:TPU:8, one launch (start us, length us, event | category | flops | bytes accessed | tf_op | source)
XLA Modules:
  0.0 53.3 jit_solution(6600569149648900047)
XLA Ops:
  0.6 0.0 copy-start
  0.6 0.0 copy-start.1
  0.7 0.0 copy-start.2
  0.7 0.0 copy-start.3
  0.7 50.8 %shard_map.86 = (f32[2,64,256]{2,1,0:T(8,128)}, f32[2,64,256]{2,1,0:T(8,128)}) custom-call(s32[2,8,256,512]{3,2,1,0:T(8,128)} %bitcast.1, f32[2,64,256]{2,1,0:T(8,128)} %re_h.1, f32[2,64,256]{2,1,0:T(8,128)} %ce_h.1, s32[2,64]{1,0:T(2,128)} %rm_h.1, s32[2,64]{1,0:T(2,128)} %cm_h.1), custom_call_target="tpu_custom_call" | custom-call | tf_op jit(solution)/shard_map/pallas_call | solution.py:490
  51.5 0.0 copy-done
  51.5 0.0 copy-done.1
  51.5 0.0 copy-done.2
  51.6 0.0 copy-done.3
  51.6 1.7 %multiply_subtract_fusion = (f32[2,64,256]{2,1,0:T(8,128)}, f32[2,64,256]{2,1,0:T(8,128)}) fusion(f32[2,64,256]{2,1,0:T(8,128)S(1)} %copy-done, f32[2,64,256]{2,1,0:T(8,128)} %get-tuple-element.5, f32[2,64,256]{2,1,0:T(8,128)S(1)} %copy-done.2, f32[2,64,256]{2,1,0:T(8,128)S(1)} %copy-done.1, f32[2,64,256]{2,1,0:T(8,128)} %get-tuple-element.4, ...), kind=kLoop, calls=%fused_computation | loop fusion | flops 262144 | bytes 1048576 | tf_op jit(solution)/shard_map/sub | solution.py:23
Async XLA Ops:
  0.6 50.9 %copy-start = (f32[2,64,256]{2,1,0:T(8,128)S(1)}, f32[2,64,256]{2,1,0:T(8,128)}, u32[]{:S(2)}) copy-start(f32[2,64,256]{2,1,0:T(8,128)} %ce_h.1) | copy-start | bytes 393220
  0.6 50.9 %copy-start.1 = (f32[2,64,256]{2,1,0:T(8,128)S(1)}, f32[2,64,256]{2,1,0:T(8,128)}, u32[]{:S(2)}) copy-start(f32[2,64,256]{2,1,0:T(8,128)} %re_h.1) | copy-start | bytes 393220
  0.7 50.9 %copy-start.2 = (f32[2,64,256]{2,1,0:T(8,128)S(1)}, f32[2,64,256]{2,1,0:T(8,128)}, u32[]{:S(2)}) copy-start(f32[2,64,256]{2,1,0:T(8,128)} %param.13) | copy-start | bytes 393220
  0.7 50.9 %copy-start.3 = (f32[2,64,256]{2,1,0:T(8,128)S(1)}, f32[2,64,256]{2,1,0:T(8,128)}, u32[]{:S(2)}) copy-start(f32[2,64,256]{2,1,0:T(8,128)} %param.12) | copy-start | bytes 393220

commit v13 on v12

--- a/solution.py
+++ b/solution.py
@@ -412,18 +412,18 @@
 
     lax.fori_loop(0, 2 * H, step, 0)
     ring(1, 3)
+    ring(0, 2)
     col_near(0)
-    ring(0, 2)
     col_far(1)
     ring(1, 2)
+    ring(0, 1)
     col_own(0)
-    ring(0, 1)
     col_near(1)
     ring(1, 1)
+    ring(0, 0)
+    ring(1, 0)
     cols_out(0)
-    ring(0, 0)
     col_own(1)
-    ring(1, 0)
     rows_out(0)
     cols_out(1)
     rows_out(1)

time: 53.7 us -> 54.3 us (1.011)
  Pallas kernels: 50.8 us -> 51.6 us
    pallas_call x1, Pallas kernels: 50.8 us -> 51.6 us  [local(): pl.pallas_call(functools.partial(kernel, NZ, XN, B, D, CB), out_shape=(ja...]
where the time goes in v13:
time: 54.3 us; the launch traced here: 54.1 us
  Pallas kernels  51.6 us (95%)
  other arithmetic  1.72 us (3%)
  between operations  0.7 us (1%)
    pallas_call x1, Pallas kernels, local(): pl.pallas_call(functools.partial(kernel, NZ, XN, B, D, CB), out_shape=(ja...  51.6 us
    sub x1, other arithmetic, adagrad(): return w - g / jnp.sqrt(a + g * g)  1.72 us

profile of v13, /device:TPU:8, one launch (start us, length us, event | category | flops | bytes accessed | tf_op | source)
XLA Modules:
  0.0 54.1 jit_solution(650157455709626566)
XLA Ops:
  0.6 0.0 copy-start
  0.6 0.0 copy-start.1
  0.7 0.0 copy-start.2
  0.7 0.0 copy-start.3
  0.7 51.6 %shard_map.86 = (f32[2,64,256]{2,1,0:T(8,128)}, f32[2,64,256]{2,1,0:T(8,128)}) custom-call(s32[2,8,256,512]{3,2,1,0:T(8,128)} %bitcast.1, f32[2,64,256]{2,1,0:T(8,128)} %re_h.1, f32[2,64,256]{2,1,0:T(8,128)} %ce_h.1, s32[2,64]{1,0:T(2,128)} %rm_h.1, s32[2,64]{1,0:T(2,128)} %cm_h.1), custom_call_target="tpu_custom_call" | custom-call | tf_op jit(solution)/shard_map/pallas_call | solution.py:490
  52.3 0.0 copy-done
  52.3 0.0 copy-done.1
  52.3 0.0 copy-done.2
  52.4 0.0 copy-done.3
  52.4 1.7 %multiply_subtract_fusion = (f32[2,64,256]{2,1,0:T(8,128)}, f32[2,64,256]{2,1,0:T(8,128)}) fusion(f32[2,64,256]{2,1,0:T(8,128)S(1)} %copy-done, f32[2,64,256]{2,1,0:T(8,128)} %get-tuple-element.5, f32[2,64,256]{2,1,0:T(8,128)S(1)} %copy-done.2, f32[2,64,256]{2,1,0:T(8,128)S(1)} %copy-done.1, f32[2,64,256]{2,1,0:T(8,128)} %get-tuple-element.4, ...), kind=kLoop, calls=%fused_computation | loop fusion | flops 262144 | bytes 1048576 | tf_op jit(solution)/shard_map/sub | solution.py:23
Async XLA Ops:
  0.6 51.7 %copy-start = (f32[2,64,256]{2,1,0:T(8,128)S(1)}, f32[2,64,256]{2,1,0:T(8,128)}, u32[]{:S(2)}) copy-start(f32[2,64,256]{2,1,0:T(8,128)} %ce_h.1) | copy-start | bytes 393220
  0.6 51.7 %copy-start.1 = (f32[2,64,256]{2,1,0:T(8,128)S(1)}, f32[2,64,256]{2,1,0:T(8,128)}, u32[]{:S(2)}) copy-start(f32[2,64,256]{2,1,0:T(8,128)} %re_h.1) | copy-start | bytes 393220
  0.7 51.7 %copy-start.2 = (f32[2,64,256]{2,1,0:T(8,128)S(1)}, f32[2,64,256]{2,1,0:T(8,128)}, u32[]{:S(2)}) copy-start(f32[2,64,256]{2,1,0:T(8,128)} %param.13) | copy-start | bytes 393220
  0.7 51.7 %copy-start.3 = (f32[2,64,256]{2,1,0:T(8,128)S(1)}, f32[2,64,256]{2,1,0:T(8,128)}, u32[]{:S(2)}) copy-start(f32[2,64,256]{2,1,0:T(8,128)} %param.12) | copy-start | bytes 393220

commit v14 on v12

--- a/solution.py
+++ b/solution.py
@@ -129,10 +129,12 @@
         tail = jnp.where(which == 0, upper, jnp.where(which == 1, lower, 0.0)).astype(BF16)
         return embed[0].astype(BF16), embed[1].astype(BF16), tail
 
-    for ref, parts in ((rows.at[0, yh, c], own_block(re, rm, 20.0)), (cols.at[yl, x], own_block(ce, cm, 0.0))):
+    def store_block(ref, parts):
         ref[0:B] = parts[0]
         ref[B : B + 16] = parts[2]
         ref[B + 16 :] = parts[1]
+
+    store_block(rows.at[0, yh, c], own_block(re, rm, 20.0))
 
     def line_of(tail):
         tail = tail.astype(F32)
@@ -328,10 +330,12 @@
         out_copy(1, s).start()
 
     for s in range(NS):
-        send(col_block(s, yl, x), col_block(s, yl, x), r_col.at[s, 0], to_yl, s)
         send(row_block(s, 0, 0), row_block(s, 0, 0), r_row.at[s, 0, 1], to_yh, s)
         send_row(s, 0, 0, True)
         send_row(s, 0, 0, False)
+        if s == 0:
+            store_block(cols.at[yl, x], own_block(ce, cm, 0.0))
+        send(col_block(s, yl, x), col_block(s, yl, x), r_col.at[s, 0], to_yl, s)
     row_step(0, 0, 1)
     col_y(0)
     row_y(0)

time: 53.7 us -> 53.5 us (level)
  no operation moved by 1% of the time
where the time goes in v14:
time: 53.5 us; the launch traced here: 53.1 us
  Pallas kernels  50.6 us (95%)
  other arithmetic  1.72 us (3%)
  between operations  0.7 us (1%)
    pallas_call x1, Pallas kernels, local(): pl.pallas_call(functools.partial(kernel, NZ, XN, B, D, CB), out_shape=(ja...  50.6 us
    sub x1, other arithmetic, adagrad(): return w - g / jnp.sqrt(a + g * g)  1.72 us

profile of v14, /device:TPU:8, one launch (start us, length us, event | category | flops | bytes accessed | tf_op | source)
XLA Modules:
  0.0 53.1 jit_solution(17741067606404575016)
XLA Ops:
  0.6 0.0 copy-start
  0.6 0.0 copy-start.1
  0.7 0.0 copy-start.2
  0.7 0.0 copy-start.3
  0.7 50.6 %shard_map.86 = (f32[2,64,256]{2,1,0:T(8,128)}, f32[2,64,256]{2,1,0:T(8,128)}) custom-call(s32[2,8,256,512]{3,2,1,0:T(8,128)} %bitcast.1, f32[2,64,256]{2,1,0:T(8,128)} %re_h.1, f32[2,64,256]{2,1,0:T(8,128)} %ce_h.1, s32[2,64]{1,0:T(2,128)} %rm_h.1, s32[2,64]{1,0:T(2,128)} %cm_h.1), custom_call_target="tpu_custom_call" | custom-call | tf_op jit(solution)/shard_map/pallas_call | solution.py:494
  51.3 0.0 copy-done
  51.3 0.0 copy-done.1
  51.3 0.0 copy-done.2
  51.3 0.0 copy-done.3
  51.3 1.7 %multiply_subtract_fusion = (f32[2,64,256]{2,1,0:T(8,128)}, f32[2,64,256]{2,1,0:T(8,128)}) fusion(f32[2,64,256]{2,1,0:T(8,128)S(1)} %copy-done, f32[2,64,256]{2,1,0:T(8,128)} %get-tuple-element.5, f32[2,64,256]{2,1,0:T(8,128)S(1)} %copy-done.2, f32[2,64,256]{2,1,0:T(8,128)S(1)} %copy-done.1, f32[2,64,256]{2,1,0:T(8,128)} %get-tuple-element.4, ...), kind=kLoop, calls=%fused_computation | loop fusion | flops 262144 | bytes 1048576 | tf_op jit(solution)/shard_map/sub | solution.py:23
Async XLA Ops:
  0.6 50.7 %copy-start = (f32[2,64,256]{2,1,0:T(8,128)S(1)}, f32[2,64,256]{2,1,0:T(8,128)}, u32[]{:S(2)}) copy-start(f32[2,64,256]{2,1,0:T(8,128)} %ce_h.1) | copy-start | bytes 393220
  0.6 50.7 %copy-start.1 = (f32[2,64,256]{2,1,0:T(8,128)S(1)}, f32[2,64,256]{2,1,0:T(8,128)}, u32[]{:S(2)}) copy-start(f32[2,64,256]{2,1,0:T(8,128)} %re_h.1) | copy-start | bytes 393220
  0.7 50.7 %copy-start.2 = (f32[2,64,256]{2,1,0:T(8,128)S(1)}, f32[2,64,256]{2,1,0:T(8,128)}, u32[]{:S(2)}) copy-start(f32[2,64,256]{2,1,0:T(8,128)} %param.13) | copy-start | bytes 393220
  0.7 50.7 %copy-start.3 = (f32[2,64,256]{2,1,0:T(8,128)S(1)}, f32[2,64,256]{2,1,0:T(8,128)}, u32[]{:S(2)}) copy-start(f32[2,64,256]{2,1,0:T(8,128)} %param.12) | copy-start | bytes 393220
